TPU v7x, 32 devices: a whole 2x2x4 slice. The times are simulated.
32 devices in a mesh: replica: 2 (over x), shard: 4 (over z), ctx: 4 (over y, core).
Axes of the slice: x: 2, y: 2, z: 4, core: 2. Of those that a mesh axis runs over, the one named last changes fastest.
Arguments:
- hidden: bfloat16 [4, 1024, 1024], P('replica', ('shard', 'ctx')), may hold values from -6 to 6
- cotangent: bfloat16 [4, 1024, 1024], P('replica', ('shard', 'ctx')), may hold values from -6 to 6
- w_qkv: bfloat16 [1024, 3072], P(('shard', 'ctx')), may hold values from -0.25 to 0.25
- w_out: bfloat16 [1024, 1024], P(('shard', 'ctx')), may hold values from -0.75 to 0.75
- w_in: bfloat16 [1024, 5248], P(('shard', 'ctx')), may hold values from -0.1875 to 0.1875
- w_down: bfloat16 [2624, 1024], P(None, ('shard', 'ctx')), may hold values from -0.25 to 0.25
- norm_attn: bfloat16 [1024], P(('shard', 'ctx')), may hold values from 0.099609375 to 1.8984375
- norm_ffn: bfloat16 [1024], P(('shard', 'ctx')), may hold values from 0.099609375 to 1.8984375
Outputs:
- block_out: bfloat16 [4, 1024, 1024], P('replica', ('shard', 'ctx'))
- grad_hidden: bfloat16 [4, 1024, 1024], P('replica', ('shard', 'ctx'))
- grad_qkv: float32 [1024, 3072], P(('shard', 'ctx'))
- grad_out_proj: float32 [1024, 1024], P(('shard', 'ctx'))
- grad_in_proj: float32 [1024, 5248], P(('shard', 'ctx'))
- grad_down_proj: float32 [2624, 1024], P(None, ('shard', 'ctx'))
- grad_norm_attn: float32 [1024], P(('shard', 'ctx'))
- grad_norm_ffn: float32 [1024], P(('shard', 'ctx'))
All inputs are finite; a program needn't handle non-finite values.
Results may differ from a plain program's by a relative error of at most 0.025.
Values may be sent and summed in bfloat16 or wider, within the bound.
A program may use at most 192 MiB of HBM per device.

v0:
```python
import jax
import jax.numpy as jnp
from jax import lax
from jax.sharding import PartitionSpec as P

HEAD_DIM = 64


norm_eps = 1e-05
rope_base = 160000.0


def layer_norm(values, scale_row):
    center = values - jnp.mean(values, axis=-1, keepdims=True)
    inverse = lax.rsqrt(jnp.mean(center * center, axis=-1, keepdims=True) + norm_eps)
    normed = center * inverse
    return (normed * scale_row, normed, inverse)


def norm_back(grad_norm, normed, inverse, scale_row):
    scaled = grad_norm * scale_row
    grad_gain = jnp.sum(grad_norm * normed, axis=0)
    grad_input = inverse * (
        scaled
        - jnp.mean(scaled, axis=-1, keepdims=True)
        - normed * jnp.mean(scaled * normed, axis=-1, keepdims=True)
    )
    return (grad_input, grad_gain)


def rope_tables(positions):
    frequency = rope_base ** (-jnp.arange(0, HEAD_DIM, 2).astype(jnp.float32) / HEAD_DIM)
    angles = positions.astype(jnp.float32)[:, None] * frequency[None, :]
    angles = jnp.concatenate([angles, angles], axis=-1)
    return (jnp.cos(angles), jnp.sin(angles))


def rotate(values, cos_table, sin_table):
    half_width = values.shape[-1] // 2
    turned = jnp.concatenate([-values[..., half_width:], values[..., :half_width]], axis=-1)
    return values * cos_table + turned * sin_table


def gate_mix(upward):
    half_width = upward.shape[1] // 2
    return jax.nn.gelu(upward[:, :half_width], approximate=False) * upward[:, half_width:]


def gram(left_side, right_side):
    return lax.dot_general(
        left_side, right_side, (((0,), (0,)), ((), ())), preferred_element_type=jnp.float32
    )


def times_back(left_side, right_side):
    return lax.dot_general(
        left_side, right_side, (((1,), (1,)), ((), ())), preferred_element_type=jnp.float32
    )


def group_count():
    return 2


def head_block(array, group_index, stride):
    part = array[:, :, group_index * stride : (group_index + 1) * stride]
    return part.reshape(part.shape[0], part.shape[1], stride // HEAD_DIM, HEAD_DIM)


def scores_of(query_block, key_block):
    return jnp.einsum(
        "bqhd,bkhd->bhqk", query_block, key_block, preferred_element_type=jnp.float32
    ) * HEAD_DIM ** (-0.5)


def attend_forward(queries, keys_all, values_all):
    groups = group_count()
    stride = queries.shape[2] // groups
    outputs = []
    totals = []
    for group_index in range(groups):
        query_block = head_block(queries, group_index, stride)
        key_block = head_block(keys_all, group_index, stride)
        value_block = head_block(values_all, group_index, stride)
        scores = scores_of(query_block, key_block)
        largest = jnp.max(scores, axis=-1, keepdims=True)
        exponent = jnp.exp(scores - largest)
        summed = jnp.sum(exponent, axis=-1, keepdims=True)
        weights = (exponent / summed).astype(jnp.bfloat16)
        blended = jnp.einsum(
            "bhqk,bkhd->bqhd", weights, value_block, preferred_element_type=jnp.float32
        )
        outputs.append(blended.reshape(blended.shape[0], blended.shape[1], stride))
        totals.append(largest + jnp.log(summed))
    return (jnp.concatenate(outputs, axis=-1).astype(jnp.bfloat16), totals)


def attend_back(queries, keys_all, values_all, grad_attended, totals):
    groups = group_count()
    stride = queries.shape[2] // groups
    query_grads = []
    key_grads = []
    value_grads = []
    for group_index in range(groups):
        query_block = head_block(queries, group_index, stride)
        key_block = head_block(keys_all, group_index, stride)
        value_block = head_block(values_all, group_index, stride)
        grad_block = head_block(grad_attended, group_index, stride)
        probs = jnp.exp(scores_of(query_block, key_block) - totals[group_index])
        grad_value = jnp.einsum(
            "bhqk,bqhd->bkhd",
            probs.astype(jnp.bfloat16),
            grad_block,
            preferred_element_type=jnp.float32,
        )
        grad_prob = jnp.einsum(
            "bqhd,bkhd->bhqk", grad_block, value_block, preferred_element_type=jnp.float32
        )
        grad_score = (
            probs * (grad_prob - jnp.sum(probs * grad_prob, axis=-1, keepdims=True))
        ).astype(jnp.bfloat16)
        grad_query = jnp.einsum(
            "bhqk,bkhd->bqhd", grad_score, key_block, preferred_element_type=jnp.float32
        ) * HEAD_DIM ** (-0.5)
        grad_key = jnp.einsum(
            "bhqk,bqhd->bkhd", grad_score, query_block, preferred_element_type=jnp.float32
        ) * HEAD_DIM ** (-0.5)
        query_grads.append(grad_query.reshape(grad_query.shape[0], grad_query.shape[1], stride))
        key_grads.append(grad_key.reshape(grad_key.shape[0], grad_key.shape[1], stride))
        value_grads.append(grad_value.reshape(grad_value.shape[0], grad_value.shape[1], stride))
    return (
        jnp.concatenate(query_grads, axis=-1),
        jnp.concatenate(key_grads, axis=-1),
        jnp.concatenate(value_grads, axis=-1),
    )


def on_device(hidden, cotangent, w_qkv, w_out, w_in, w_down, norm_attn, norm_ffn):
    sequences, local_len, features = hidden.shape
    row_count = sequences * local_len
    head_count = features // HEAD_DIM
    qkv_full, out_full, gain_one = (
        lax.all_gather(w_qkv, ("shard", "ctx"), axis=0, tiled=True),
        lax.all_gather(w_out, ("shard", "ctx"), axis=0, tiled=True),
        lax.all_gather(norm_attn, ("shard", "ctx"), axis=0, tiled=True),
    )
    in_full, down_full, gain_two = (
        lax.all_gather(w_in, ("shard", "ctx"), axis=0, tiled=True),
        lax.all_gather(w_down, ("shard", "ctx"), axis=1, tiled=True),
        lax.all_gather(norm_ffn, ("shard", "ctx"), axis=0, tiled=True),
    )
    gain_attn = gain_one.astype(jnp.float32)
    gain_ffn = gain_two.astype(jnp.float32)
    flat_in = hidden.reshape(row_count, features).astype(jnp.float32)
    normed_one, centered_one, inverse_one = layer_norm(flat_in, gain_attn)
    first = normed_one.astype(jnp.bfloat16)
    packed = jnp.dot(first, qkv_full, preferred_element_type=jnp.float32)
    packed = packed.reshape(sequences, local_len, 3, head_count, HEAD_DIM)
    positions = lax.axis_index(("shard", "ctx")) * local_len + jnp.arange(
        local_len, dtype=jnp.int32
    )
    cos_table, sin_table = rope_tables(positions)
    cos_table = cos_table[None, :, None, :]
    sin_table = sin_table[None, :, None, :]

    def turn_pair(query_pre, key_pre):
        return (rotate(query_pre, cos_table, sin_table), rotate(key_pre, cos_table, sin_table))

    (query_rot, key_rot), turn_back = jax.vjp(turn_pair, packed[:, :, 0], packed[:, :, 1])
    queries = query_rot.reshape(sequences, local_len, features).astype(jnp.bfloat16)
    keys_local = key_rot.reshape(sequences, local_len, features).astype(jnp.bfloat16)
    values_local = packed[:, :, 2].reshape(sequences, local_len, features).astype(jnp.bfloat16)
    keys_all, values_all = (
        lax.all_gather(keys_local, ("shard", "ctx"), axis=1, tiled=True),
        lax.all_gather(values_local, ("shard", "ctx"), axis=1, tiled=True),
    )
    attended, totals = attend_forward(queries, keys_all, values_all)
    attended_low = attended.reshape(row_count, features)
    residual = flat_in + jnp.dot(attended_low, out_full, preferred_element_type=jnp.float32)
    normed_two, centered_two, inverse_two = layer_norm(residual, gain_ffn)
    second = normed_two.astype(jnp.bfloat16)
    upward = jnp.dot(second, in_full, preferred_element_type=jnp.float32)
    gated, gate_back = jax.vjp(gate_mix, upward)
    gated_low = gated.astype(jnp.bfloat16)
    output = residual + jnp.dot(gated_low, down_full, preferred_element_type=jnp.float32)
    block_out = output.astype(jnp.bfloat16).reshape(hidden.shape)
    qkv_back, out_back, gain_one_back = (
        lax.all_gather(w_qkv, ("shard", "ctx"), axis=0, tiled=True),
        lax.all_gather(w_out, ("shard", "ctx"), axis=0, tiled=True),
        lax.all_gather(norm_attn, ("shard", "ctx"), axis=0, tiled=True),
    )
    in_back, down_back, gain_two_back = (
        lax.all_gather(w_in, ("shard", "ctx"), axis=0, tiled=True),
        lax.all_gather(w_down, ("shard", "ctx"), axis=1, tiled=True),
        lax.all_gather(norm_ffn, ("shard", "ctx"), axis=0, tiled=True),
    )
    gain_attn_back = gain_one_back.astype(jnp.float32)
    gain_ffn_back = gain_two_back.astype(jnp.float32)
    grad_top = cotangent.reshape(row_count, features)
    grad_gated = times_back(grad_top, down_back)
    grad_up = gate_back(grad_gated)[0].astype(jnp.bfloat16)
    grad_second = times_back(grad_up, in_back)
    grad_norm_two, grad_gain_ffn = norm_back(grad_second, centered_two, inverse_two, gain_ffn_back)
    grad_resid = grad_top.astype(jnp.float32) + grad_norm_two
    grad_attn = grad_resid.astype(jnp.bfloat16)
    grad_attended = times_back(grad_attn, out_back).astype(jnp.bfloat16)
    grad_attended = grad_attended.reshape(sequences, local_len, features)
    grad_query, grad_key, grad_value = attend_back(
        queries, keys_all, values_all, grad_attended, totals
    )
    grad_key_own, grad_value_own = (
        lax.psum_scatter(
            grad_key.astype(jnp.bfloat16), ("shard", "ctx"), scatter_dimension=1, tiled=True
        ).astype(jnp.float32),
        lax.psum_scatter(
            grad_value.astype(jnp.bfloat16), ("shard", "ctx"), scatter_dimension=1, tiled=True
        ).astype(jnp.float32),
    )
    head_shape = (sequences, local_len, head_count, HEAD_DIM)
    grad_query_pre, grad_key_pre = turn_back(
        (grad_query.reshape(head_shape), grad_key_own.reshape(head_shape))
    )
    grad_packed = jnp.stack(
        [grad_query_pre, grad_key_pre, grad_value_own.reshape(head_shape)], axis=2
    )
    grad_packed = grad_packed.reshape(row_count, 3 * features).astype(jnp.bfloat16)
    grad_first = times_back(grad_packed, qkv_back)
    grad_norm_one, grad_gain_attn = norm_back(grad_first, centered_one, inverse_one, gain_attn_back)
    grad_hidden = (grad_resid + grad_norm_one).astype(jnp.bfloat16).reshape(hidden.shape)
    pieces = (
        lax.psum_scatter(
            gram(first, grad_packed).astype(jnp.bfloat16),
            ("shard", "ctx"),
            scatter_dimension=0,
            tiled=True,
        ).astype(jnp.float32),
        lax.psum_scatter(
            gram(attended_low, grad_attn).astype(jnp.bfloat16),
            ("shard", "ctx"),
            scatter_dimension=0,
            tiled=True,
        ).astype(jnp.float32),
        lax.psum_scatter(
            gram(second, grad_up).astype(jnp.bfloat16),
            ("shard", "ctx"),
            scatter_dimension=0,
            tiled=True,
        ).astype(jnp.float32),
        lax.psum_scatter(
            gram(gated_low, grad_top).astype(jnp.bfloat16),
            ("shard", "ctx"),
            scatter_dimension=1,
            tiled=True,
        ).astype(jnp.float32),
        lax.psum_scatter(
            grad_gain_attn.astype(jnp.bfloat16), ("shard", "ctx"), scatter_dimension=0, tiled=True
        ).astype(jnp.float32),
        lax.psum_scatter(
            grad_gain_ffn.astype(jnp.bfloat16), ("shard", "ctx"), scatter_dimension=0, tiled=True
        ).astype(jnp.float32),
    )
    summed = (
        lax.psum(pieces[0].astype(jnp.bfloat16), "replica").astype(jnp.float32),
        lax.psum(pieces[1].astype(jnp.bfloat16), "replica").astype(jnp.float32),
        lax.psum(pieces[2].astype(jnp.bfloat16), "replica").astype(jnp.float32),
        lax.psum(pieces[3].astype(jnp.bfloat16), "replica").astype(jnp.float32),
        lax.psum(pieces[4].astype(jnp.bfloat16), "replica").astype(jnp.float32),
        lax.psum(pieces[5].astype(jnp.bfloat16), "replica").astype(jnp.float32),
    )
    return (
        block_out,
        grad_hidden,
        summed[0],
        summed[1],
        summed[2],
        summed[3],
        summed[4],
        summed[5],
    )


def solution(mesh):
    placed = (
        P("replica", ("shard", "ctx"), None),
        P("replica", ("shard", "ctx"), None),
        P(("shard", "ctx"), None),
        P(("shard", "ctx"), None),
        P(("shard", "ctx"), None),
        P(None, ("shard", "ctx")),
        P(("shard", "ctx")),
        P(("shard", "ctx")),
    )
    return jax.shard_map(
        on_device,
        mesh=mesh,
        in_specs=placed,
        out_specs=(
            P("replica", ("shard", "ctx"), None),
            P("replica", ("shard", "ctx"), None),
            P(("shard", "ctx"), None),
            P(("shard", "ctx"), None),
            P(("shard", "ctx"), None),
            P(None, ("shard", "ctx")),
            P(("shard", "ctx")),
            P(("shard", "ctx")),
        ),
        check_vma=False,
    )
```

profile of v0, /device:TPU:0, one launch (start us, length us, event | category | flops | bytes accessed | tf_op | source)
XLA Modules:
  0.0 1063.5 jit_solution(4428444646715613096)
XLA Ops:
  8.0 1.3 fusion.59
  11.6 35.2 %all-reduce.13 = (bf16[1024]{0:T(1024)(128)(2,1)S(1)}, bf16[1024]{0:T(1024)(128)(2,1)S(1)}) all-reduce(bf16[1024]{0:T(1024)(128)(2,1)S(1)} %dynamic-update-slice, bf16[1024]{0:T(1024)(128)(2,1)S(1)} %dynamic-update-slice.1), channel_id=1, replica_groups=mesh['replica'=2,'shard'=4,'ctx'=4] {'shard','ctx'}, use_global_device_ids=true, to_apply=%add.6 | all-reduce | flops 2048 | bytes 8192
  50.3 24.8 %all-gather.7.cloned.1.call-done = bf16[1024,3072]{1,0:T(8,128)(2,1)} async-done(((bf16[64,3072]{1,0:T(8,128)(2,1)}), bf16[1024,3072]{1,0:T(8,128)(2,1)}) %all-gather.7.cloned.1.call-update) | async-done | bytes 6291472 | tf_op jit(solution)/shard_map/all_gather | solution.py:143
  75.1 8.6 copy.76
  83.7 4.5 fusion.37
  88.2 1.7 copy-done.25
  93.1 3.0 fusion.54
  102.2 1.9 add_convert_fusion.2
  106.3 34.0 %all-gather.9.cloned.1.call-done = bf16[2,1024,1024]{2,0,1:T(2,128)(2,1)} async-done(((bf16[2,64,1024]{2,0,1:T(2,128)(2,1)}), bf16[2,1024,1024]{2,0,1:T(2,128)(2,1)}) %all-gather.9.cloned.1.call-update) | async-done | bytes 4194320 | tf_op jit(solution)/shard_map/all_gather | solution.py:175
  140.3 5.7 fusion.53
  146.0 6.2 copy.88
  152.2 4.7 copy.78
  156.9 35.3 %all-gather.11.cloned.1.call-done = bf16[2,1024,1024]{2,1,0:T(8,128)(2,1)} async-done(((bf16[2,64,1024]{2,1,0:T(8,128)(2,1)}), bf16[2,1024,1024]{2,1,0:T(8,128)(2,1)}) %all-gather.11.cloned.1.call-update) | async-done | bytes 4194320 | tf_op jit(solution)/shard_map/all_gather | solution.py:174
  192.2 4.5 fusion.52
  196.7 3.0 copy.89
  199.7 5.1 copy.85
  204.8 2.4 multiply_reduce_fusion.3
  210.3 1.3 fusion.32
  216.0 1.3 fusion.33
  217.7 16.4 %all-gather.13.cloned.1.call-done = bf16[1024,1024]{1,0:T(8,128)(2,1)} async-done(((bf16[64,1024]{1,0:T(8,128)(2,1)}), bf16[1024,1024]{1,0:T(8,128)(2,1)}) %all-gather.13.cloned.1.call-update) | async-done | bytes 2097168 | tf_op jit(solution)/shard_map/all_gather | solution.py:144
  234.1 2.1 fusion.60
  237.1 87.4 %all-gather.15.cloned.1.call-done = bf16[1024,5248]{1,0:T(8,128)(2,1)} async-done(((bf16[64,5248]{1,0:T(8,128)(2,1)}), bf16[1024,5248]{1,0:T(8,128)(2,1)}) %all-gather.15.cloned.1.call-update) | async-done | bytes 10747920 | tf_op jit(solution)/shard_map/all_gather | solution.py:148
  324.5 7.4 fusion.50
  332.0 50.3 %all-gather.17.cloned.1.call-done = bf16[2624,1024]{0,1:T(8,128)(2,1)} async-done(((bf16[2624,64]{0,1:T(8,128)(2,1)}), bf16[2624,1024]{0,1:T(8,128)(2,1)}) %all-gather.17.cloned.1.call-update) | async-done | bytes 5373968 | tf_op jit(solution)/shard_map/all_gather | solution.py:149
  382.3 6.8 fusion.36
  389.1 1.8 multiply_add_fusion
  390.9 5.0 multiply_reduce_fusion.4
  396.0 1.3 multiply_add_fusion.1
  398.4 3.3 fusion.17
  402.5 4.0 multiply_reduce_fusion
  406.7 4.6 fusion.14
  411.3 3.5 multiply_reduce_fusion.1
  414.7 4.0 copy.106
  418.8 4.0 multiply_convert_fusion.2
  422.8 2.0 multiply_convert_fusion
  424.8 6.2 copy.99
  431.0 6.2 copy.105
  437.2 4.0 multiply_convert_fusion.3
  441.2 2.0 multiply_convert_fusion.1
  443.2 6.4 copy.98
  449.6 8.0 pad_maximum_fusion.1
  457.6 8.0 pad_maximum_fusion
  466.6 3.1 convolution_convert_fusion.3
  469.8 5.3 convolution_convert_fusion.1
  476.1 3.2 fusion.26
  480.1 154.6 %all-reduce.20.cloned.1.call-done = (bf16[2,1024,1024]{2,0,1:T(2,128)(2,1)}, bf16[2,1024,1024]{2,0,1:T(2,128)(2,1)}) async-done(((bf16[2,1024,1024]{2,0,1:T(2,128)(2,1)}, bf16[2,1024,1024]{2,0,1:T(2,128)(2,1)}), (bf16[2,1024,1024]{2,0,1:T(2,128)(2,1)}, bf16[2,1024,1024]{2,0,1:T(2,128)(2,1)})) %all-reduce.20.cloned.1.call-update) | async-done | bytes 8388624
  638.9 1.4 copy.113
  642.7 2.2 copy.109
  644.9 2.3 convert_element_type.185
  647.2 4.4 convolution_convert_fusion.2
  651.7 1.3 copy-done.9
  653.0 7.2 convolution_convert_fusion
  661.0 39.3 %reduce-scatter.7.cloned.1.call-done = bf16[64,1024]{1,0:T(8,128)(2,1)} async-done(((bf16[1024,1024]{1,0:T(8,128)(2,1)}), bf16[64,1024]{1,0:T(8,128)(2,1)}) %reduce-scatter.7.cloned.1.call-update) | async-done | bytes 131088 | tf_op jit(solution)/shard_map/reduce_scatter | solution.py:237
  700.3 82.9 %reduce-scatter.11.cloned.1.call-done = bf16[2624,64]{0,1:T(8,128)(2,1)} async-done(((bf16[2624,1024]{0,1:T(8,128)(2,1)}), bf16[2624,64]{0,1:T(8,128)(2,1)}) %reduce-scatter.11.cloned.1.call-update) | async-done | bytes 335888 | tf_op jit(solution)/shard_map/reduce_scatter | solution.py:249
  783.3 88.6 %reduce-scatter.5.cloned.1.call-done = bf16[64,3072]{1,0:T(8,128)(2,1)} async-done(((bf16[1024,3072]{1,0:T(8,128)(2,1)}), bf16[64,3072]{1,0:T(8,128)(2,1)}) %reduce-scatter.5.cloned.1.call-update) | async-done | bytes 393232 | tf_op jit(solution)/shard_map/reduce_scatter | solution.py:231
  871.9 124.2 %reduce-scatter.9.cloned.1.call-done = bf16[64,5248]{1,0:T(8,128)(2,1)} async-done(((bf16[1024,5248]{1,0:T(8,128)(2,1)}), bf16[64,5248]{1,0:T(8,128)(2,1)}) %reduce-scatter.9.cloned.1.call-update) | async-done | bytes 671760 | tf_op jit(solution)/shard_map/reduce_scatter | solution.py:243
  996.1 5.2 fusion.31
  1001.3 5.6 multiply_reduce_fusion.5
  1006.9 31.8 %all-reduce.12 = (bf16[1024]{0:T(1024)(128)(2,1)S(1)}, bf16[1024]{0:T(1024)(128)(2,1)S(1)}) all-reduce(bf16[1024]{0:T(1024)(128)(2,1)S(1)} %get-tuple-element.10, bf16[1024]{0:T(1024)(128)(2,1)S(1)} %copy-done.50), channel_id=8, replica_groups=mesh['replica'=2,'shard'=4,'ctx'=4] {'shard','ctx'}, use_global_device_ids=true, to_apply=%region_25.0.clone | all-reduce | flops 2048 | bytes 8192
  1038.9 5.0 all-reduce.15
  1045.9 3.7 all-reduce.22.cloned.1.call-done
  1049.6 1.7 convert_element_type.191
  1051.3 1.9 convert_element_type.189
  1053.2 1.9 convert_element_type.195
  (209 shorter events, 40.7 us)
Async XLA Ops:
  7.2 67.9 %all-gather.7.cloned.1.call-start = ((), (), s32[]{:S(2)}) async-start(), calls=%async_computation.4 | async-start | bytes 6684672 | tf_op jit(solution)/shard_map/all_gather | solution.py:143
  7.9 132.4 %all-gather.9.cloned.1.call-start = ((), (), s32[]{:S(2)}) async-start(), calls=%async_computation.5 | async-start | bytes 4456448 | tf_op jit(solution)/shard_map/all_gather | solution.py:175
  47.9 35.7 %copy-start.48 = (f32[2,64]{1,0:T(2,128)}, f32[2,64]{1,0:T(2,128)S(1)}, u32[]{:S(2)}) copy-start(f32[2,64]{1,0:T(2,128)S(1)} %broadcast_multiply_fusion.2) | copy-start | bytes 1540
  49.1 34.5 %copy-start.51 = (f32[2,64]{1,0:T(2,128)}, f32[2,64]{1,0:T(2,128)S(1)}, u32[]{:S(2)}) copy-start(f32[2,64]{1,0:T(2,128)S(1)} %add_rsqrt_fusion) | copy-start | bytes 1540
  50.3 33.4 %copy-start.32 = (bf16[2,64,1024]{2,1,0:T(8,128)(2,1)}, bf16[2,64,1024]{2,1,0:T(8,128)(2,1)S(1)}, u32[]{:S(2)}) copy-start(bf16[2,64,1024]{2,1,0:T(8,128)(2,1)S(1)} %multiply_convert_fusion.6) | copy-start | bytes 786436
  88.2 1.7 copy-start.25
  91.0 101.2 %all-gather.11.cloned.1.call-start = ((), (), s32[]{:S(2)}) async-start(), calls=%async_computation.6 | async-start | bytes 4456448 | tf_op jit(solution)/shard_map/all_gather | solution.py:174
  97.2 1.2 copy-start.22
  99.6 1.0 copy-start.29
  100.1 2.1 copy-start.26
  100.1 2.1 copy-start.27
  104.1 130.0 %all-gather.13.cloned.1.call-start = ((), (), s32[]{:S(2)}) async-start(), calls=%async_computation.7 | async-start | bytes 2228224 | tf_op jit(solution)/shard_map/all_gather | solution.py:144
  104.7 219.9 %all-gather.15.cloned.1.call-start = ((), (), s32[]{:S(2)}) async-start(), calls=%async_computation.8 | async-start | bytes 11419648 | tf_op jit(solution)/shard_map/all_gather | solution.py:148
  105.3 277.0 %all-gather.17.cloned.1.call-start = ((), (), s32[]{:S(2)}) async-start(), calls=%async_computation.9 | async-start | bytes 5849088 | tf_op jit(solution)/shard_map/all_gather | solution.py:149
  105.8 528.9 %all-reduce.20.cloned.1.call-start = ((), (), s32[]{:S(2)}) async-start(), calls=%async_computation.14 | async-start | bytes 16777216
  106.1 105.9 %copy-start.23 = (bf16[2,64,512]{1,2,0:T(8,128)(2,1)}, bf16[2,64,512]{1,2,0:T(8,128)(2,1)S(1)}, u32[]{:S(2)}) copy-start(bf16[2,64,512]{1,2,0:T(8,128)(2,1)S(1)} %copy.115) | copy-start | bytes 393220
  199.7 12.4 %copy-start.6 = (bf16[2,1024,512]{1,2,0:T(8,128)(2,1)}, bf16[2,1024,512]{1,2,0:T(8,128)(2,1)S(1)}, u32[]{:S(2)}) copy-start(bf16[2,1024,512]{1,2,0:T(8,128)(2,1)S(1)} %copy.89) | copy-start | bytes 6291460
  207.2 2.1 copy-start
  207.2 3.1 copy-start.14
  212.9 2.1 copy-start.2
  212.9 3.1 copy-start.16
  216.0 18.1 %copy-start.11 = (bf16[2,64,1024]{2,1,0:T(8,128)(2,1)S(1)}, bf16[2,64,1024]{2,1,0:T(8,128)(2,1)}, u32[]{:S(2)}) copy-start(bf16[2,64,1024]{2,1,0:T(8,128)(2,1)} %param.8) | copy-start | bytes 786436
  217.7 19.4 %copy-start.30 = (bf16[128,1024]{1,0:T(8,128)(2,1)}, bf16[128,1024]{1,0:T(8,128)(2,1)S(1)}, u32[]{:S(2)}) copy-start(bf16[128,1024]{1,0:T(8,128)(2,1)S(1)} %constant_dynamic-update-slice_fusion) | copy-start | bytes 786436
  236.2 159.7 %copy-start.44 = (f32[128]{0:T(128)}, f32[128]{0:T(128)S(1)}, u32[]{:S(2)}) copy-start(f32[128]{0:T(128)S(1)} %broadcast_multiply_fusion.7) | copy-start | bytes 1540
  236.5 159.5 %copy-start.46 = (f32[128]{0:T(128)}, f32[128]{0:T(128)S(1)}, u32[]{:S(2)}) copy-start(f32[128]{0:T(128)S(1)} %add_rsqrt_fusion.1) | copy-start | bytes 1540
  324.5 66.4 %slice-start = ((s8[10747904]{0:T(1024)(128)(4,1)}), s8[2359296]{0:T(1024)(128)(4,1)S(1)}, s32[]{:S(2)}) async-start(s8[10747904]{0:T(1024)(128)(4,1)} %bitcast.114), calls=%async_computation.16 | async-start | bytes 4718592
  382.3 6.8 copy-start.10
  382.3 8.6 slice-start.1
  382.3 8.6 slice-start.2
  389.0 1.9 copy-start.20
  390.9 5.0 copy-start.8
  390.9 5.0 copy-start.34
  390.9 6.3 copy-start.13
  397.3 0.9 copy-start.18
  398.3 3.5 copy-start.3
  398.3 4.1 copy-start.17
  398.4 4.1 copy-start.41
  406.7 4.6 copy-start.1
  406.7 4.6 copy-start.15
  414.7 4.0 copy-start.42
  414.7 4.0 copy-start.43
  418.8 4.1 copy-start.24
  441.2 2.0 copy-start.4
  465.6 0.9 copy-start.31
  465.6 4.1 copy-start.35
  465.7 234.7 %reduce-scatter.7.cloned.1.call-start = ((), (), s32[]{:S(2)}) async-start(), calls=%async_computation.11 | async-start | bytes 2228224 | tf_op jit(solution)/shard_map/reduce_scatter | solution.py:237
  469.7 313.5 %reduce-scatter.11.cloned.1.call-start = ((), (), s32[]{:S(2)}) async-start(), calls=%async_computation.13 | async-start | bytes 5849088 | tf_op jit(solution)/shard_map/reduce_scatter | solution.py:249
  475.1 396.7 %reduce-scatter.5.cloned.1.call-start = ((), (), s32[]{:S(2)}) async-start(), calls=%async_computation.10 | async-start | bytes 6684672 | tf_op jit(solution)/shard_map/reduce_scatter | solution.py:231
  476.1 3.3 copy-start.5
  476.1 3.3 copy-start.7
  635.8 4.4 copy-start.21
  635.9 4.4 copy-start.40
  640.5 0.8 copy-start.38
  641.3 1.0 copy-start.28
  642.7 4.5 copy-start.33
  651.6 1.4 copy-start.9
  651.6 1.4 copy-start.45
  651.6 1.4 copy-start.47
  651.7 344.5 %reduce-scatter.9.cloned.1.call-start = ((), (), s32[]{:S(2)}) async-start(), calls=%async_computation.12 | async-start | bytes 11419648 | tf_op jit(solution)/shard_map/reduce_scatter | solution.py:243
  660.2 336.0 %copy-start.12 = (bf16[128,2624]{1,0:T(8,128)(2,1)S(1)}, bf16[128,2624]{1,0:T(8,128)(2,1)}, u32[]{:S(2)}) copy-start(bf16[128,2624]{1,0:T(8,128)(2,1)} %get-tuple-element.33) | copy-start | bytes 2015236
  660.2 389.4 %all-reduce.22.cloned.1.call-start = ((), (), s32[]{:S(2)}) async-start(), calls=%async_computation.15 | async-start | bytes 3080192 | tf_op jit(solution)/shard_map/psum | solution.py:263
  1001.3 5.6 copy-start.50
  1001.3 43.6 %copy-start.19 = (f32[128,1024]{1,0:T(8,128)S(1)}, f32[128,1024]{1,0:T(8,128)}, u32[]{:S(2)}) copy-start(f32[128,1024]{1,0:T(8,128)} %copy-done.18) | copy-start | bytes 1572868
  1049.6 5.5 copy-start.36
  (4 other events, 2.6 us)
Sparse Core Ops, SparseCore 0:
  10.3 64.7 all-gather.6
  91.1 49.1 all-gather.8
  143.1 49.0 all-gather.10
  194.2 39.8 all-gather.12
  236.2 88.2 all-gather.14
  326.7 55.5 all-gather.16
  465.8 168.9 all-reduce.19
  638.9 61.3 reduce-scatter.6
  704.2 78.9 reduce-scatter.10
  787.6 84.2 reduce-scatter.4
  876.0 120.1 reduce-scatter.8
  998.5 51.1 all-reduce.21
where the time goes:
time: 1070 us; the launch traced here: 1060 us
  waiting for transfers between devices  744 us (70%)
  local copies, waits for them, and re-layouts  94.9 us (9%)
  matrix products  86.5 us (8%)
  blocking collectives  72 us (7%)
  other arithmetic  48.5 us (5%)
  between operations  16.8 us (2%)
    unnamed x13, waiting for transfers between devices  157 us
    reduce_scatter x1, waiting for transfers between devices, on_device(): lax.psum_scatter(gram(second, grad_up).astype(jnp.bfloat16), ('shard', 'c...  124 us
    reduce_scatter x1, waiting for transfers between devices, on_device(): lax.psum_scatter(gram(first, grad_packed).astype(jnp.bfloat16), ('shard',...  88.6 us
    all_gather x1, waiting for transfers between devices, on_device(): lax.all_gather(w_in, ('shard', 'ctx'), axis=0, tiled=True)  87.4 us
    reduce_scatter x1, waiting for transfers between devices, on_device(): lax.psum_scatter(gram(gated_low, grad_top).astype(jnp.bfloat16), ('shard'...  82.9 us
    unnamed x2, blocking collectives  67.1 us
    all_gather x1, waiting for transfers between devices, on_device(): lax.all_gather(w_down, ('shard', 'ctx'), axis=1, tiled=True)  50.3 us
    reduce_scatter x1, waiting for transfers between devices, on_device(): lax.psum_scatter(gram(attended_low, grad_attn).astype(jnp.bfloat16), ('sh...  39.3 us
  transfers between devices with their start and end apart: 12, of which 12 were waited for; matrix products, arithmetic and copies ran while one was open for 11% of the time, Pallas kernels for 0%

commit v1 on v0

v1 whole, which is shorter than its diff:
```python
import jax
import jax.numpy as jnp
import numpy as np
from jax import lax
from jax.experimental import pallas as pl
from jax.experimental.pallas import tpu as pltpu
from jax.sharding import Mesh, PartitionSpec as P

HEAD_DIM = 64
norm_eps = 1e-05
rope_base = 160000.0
f32 = jnp.float32
bf16 = jnp.bfloat16
CHIPS = ("shard", "cy")
WIDE = 128
BLOCK = 256


def layer_norm(values, scale_row):
    center = values - jnp.mean(values, axis=-1, keepdims=True)
    inverse = lax.rsqrt(jnp.mean(center * center, axis=-1, keepdims=True) + norm_eps)
    normed = center * inverse
    return (normed * scale_row, normed, inverse)


def norm_back(grad_norm, normed, inverse, scale_row):
    scaled = grad_norm * scale_row
    grad_gain = jnp.sum(grad_norm * normed, axis=0)
    grad_input = inverse * (
        scaled
        - jnp.mean(scaled, axis=-1, keepdims=True)
        - normed * jnp.mean(scaled * normed, axis=-1, keepdims=True)
    )
    return (grad_input, grad_gain)


def dot_nn(a, b):
    return lax.dot_general(a, b, (((1,), (0,)), ((), ())), preferred_element_type=f32)


def dot_nt(a, b):
    return lax.dot_general(a, b, (((1,), (1,)), ((), ())), preferred_element_type=f32)


def dot_tn(a, b):
    return lax.dot_general(a, b, (((0,), (0,)), ((), ())), preferred_element_type=f32)


def rope_tables(length):
    frequency = rope_base ** (-np.arange(0, HEAD_DIM, 2, dtype=np.float32) / HEAD_DIM)
    blocks = np.arange(length).reshape(-1, 2, HEAD_DIM)
    orders = np.stack([blocks.reshape(-1), blocks[:, ::-1].reshape(-1)])
    angles = orders.astype(np.float32)[:, :, None] * frequency.astype(np.float32)
    cos = np.tile(np.cos(angles), (1, 1, 4)).astype(np.float32)
    sin = np.sin(angles).astype(np.float32)
    sin = np.concatenate([-sin, sin, -sin, sin], axis=-1)
    return cos, sin


def swap_halves(values):
    lane = lax.broadcasted_iota(jnp.int32, values.shape, 1)
    low = lax.rem(lane, HEAD_DIM) < HEAD_DIM // 2
    return jnp.where(low, pltpu.roll(values, WIDE - 32, 1), pltpu.roll(values, 32, 1))


def head_only(values, head):
    lane = lax.broadcasted_iota(jnp.int32, values.shape, 1)
    inside = (lane < HEAD_DIM) if head == 0 else (lane >= HEAD_DIM)
    return jnp.where(inside, values, jnp.zeros_like(values))


def join_heads(first, second):
    lane = lax.broadcasted_iota(jnp.int32, first.shape, 1)
    return jnp.where(lane < HEAD_DIM, first, second)


def attend_kernel(first, w_qkv, w_out, cos, sin, part, q, k, v, att, lse):
    tokens = first.shape[0]

    @pl.loop(0, tokens // BLOCK)
    def _(i):
        rows = pl.ds(pl.multiple_of(i * BLOCK, BLOCK), BLOCK)
        packed = dot_nn(first[rows, :], w_qkv[...])
        c, s = cos[rows, :], sin[rows, :]
        pq, pk = packed[:, :WIDE], packed[:, WIDE : 2 * WIDE]
        q[rows, :] = (pq * c + swap_halves(pq) * s).astype(bf16)
        k[rows, :] = (pk * c + swap_halves(pk) * s).astype(bf16)
        v[rows, :] = packed[:, 2 * WIDE :].astype(bf16)

    @pl.loop(0, tokens // BLOCK)
    def _(i):
        rows = pl.ds(pl.multiple_of(i * BLOCK, BLOCK), BLOCK)
        q_rows = q[rows, :]
        outs = []
        for head in range(2):
            scores = dot_nt(head_only(q_rows, head), k[...]) * HEAD_DIM**-0.5
            top = jnp.max(scores, axis=-1, keepdims=True)
            exponent = jnp.exp(scores - top)
            total = jnp.sum(exponent, axis=-1, keepdims=True)
            weights = (exponent * (1.0 / total)).astype(bf16)
            outs.append(dot_nn(weights, v[...]))
            lse[rows, head : head + 1] = top + jnp.log(total)
        joined = join_heads(*outs).astype(bf16)
        att[rows, :] = joined
        part[rows, :] = dot_nn(joined, w_out[...]).astype(bf16)


def attend_back_kernel(
    branch, first, w_qkv, w_out, cos, sin, q, k, v, att, lse,
    part, grad_qkv, grad_out, dpacked, dk, dv,
):
    tokens = branch.shape[0]
    dk[...] = jnp.zeros_like(dk)
    dv[...] = jnp.zeros_like(dv)

    @pl.loop(0, tokens // BLOCK)
    def _(i):
        rows = pl.ds(pl.multiple_of(i * BLOCK, BLOCK), BLOCK)
        grad = dot_nt(branch[rows, :], w_out[...]).astype(bf16)
        q_rows = q[rows, :]
        dqs, dks, dvs = [], [], []
        for head in range(2):
            scores = dot_nt(head_only(q_rows, head), k[...]) * HEAD_DIM**-0.5
            probs = jnp.exp(scores - lse[rows, head : head + 1])
            dvs.append(dot_tn(probs.astype(bf16), grad))
            dprobs = dot_nt(head_only(grad, head), v[...])
            dot_sum = jnp.sum(probs * dprobs, axis=-1, keepdims=True)
            dscores = (probs * (dprobs - dot_sum)).astype(bf16)
            dqs.append(dot_nn(dscores, k[...]))
            dks.append(dot_tn(dscores, q_rows))
        dk[...] += join_heads(*dks)
        dv[...] += join_heads(*dvs)
        dq = join_heads(*dqs) * HEAD_DIM**-0.5
        dq = dq * cos[rows, :] - swap_halves(dq) * sin[rows, :]
        dpacked[rows, :WIDE] = dq.astype(bf16)

    @pl.loop(0, tokens // BLOCK)
    def _(i):
        rows = pl.ds(pl.multiple_of(i * BLOCK, BLOCK), BLOCK)
        d = dk[rows, :] * HEAD_DIM**-0.5
        d = d * cos[rows, :] - swap_halves(d) * sin[rows, :]
        dpacked[rows, WIDE : 2 * WIDE] = d.astype(bf16)
        dpacked[rows, 2 * WIDE :] = dv[rows, :].astype(bf16)
        part[rows, :] = dot_nt(dpacked[rows, :], w_qkv[...]).astype(bf16)

    grad_out[...] = dot_tn(att[...], branch[...]).astype(bf16)

    @pl.loop(0, first.shape[1] // BLOCK)
    def _(i):
        cols = pl.ds(pl.multiple_of(i * BLOCK, BLOCK), BLOCK)
        grad_qkv[cols, :] = dot_tn(first[:, cols], dpacked[...]).astype(bf16)


def call(kernel, outs, scratch, *args):
    vmem = pl.BlockSpec(memory_space=pltpu.VMEM)
    return pl.pallas_call(
        kernel,
        out_shape=[jax.ShapeDtypeStruct(s, d) for s, d in outs],
        in_specs=[vmem] * len(args),
        out_specs=[vmem] * len(outs),
        scratch_shapes=[pltpu.VMEM(s, d) for s, d in scratch],
        compiler_params=pltpu.CompilerParams(vmem_limit_bytes=48 * 2**20),
    )(*args)


def gate_mix(upward):
    half_width = upward.shape[1] // 2
    return jax.nn.gelu(upward[:, :half_width], approximate=False) * upward[:, half_width:]


def swap_core(value):
    return lax.ppermute(value, "core", [(0, 1), (1, 0)])


def on_device(replicas, chips, hidden, cotangent, w_qkv, w_out, w_in, w_down, norm_attn, norm_ffn):
    _, local_len, features = hidden.shape
    units = w_down.shape[0] // chips
    core = lax.axis_index("core")
    take = lambda value, axis, index: lax.dynamic_index_in_dim(value, index, axis, keepdims=False)

    gains = lax.all_gather(
        jnp.stack([norm_attn, norm_ffn]), CHIPS + ("core",), axis=1, tiled=True
    ).astype(f32)
    other = swap_core(jnp.stack([take(hidden, 0, 1 - core), take(cotangent, 0, 1 - core)]))
    x = jnp.concatenate([take(hidden, 0, core), other[0]]).astype(f32)
    grad_top = jnp.concatenate([take(cotangent, 0, core), other[1]])

    def spread(blocks):
        moved = lax.all_to_all(blocks, CHIPS, 0, 0, tiled=True)
        both = lax.all_gather(moved, "core", axis=1, tiled=True)
        return both.reshape(features, blocks.shape[-1])

    rows = w_qkv.shape[0]
    qkv_own = spread(
        w_qkv.reshape(rows, 3, chips, WIDE).transpose(2, 0, 1, 3).reshape(chips, rows, 3 * WIDE)
    )
    ffn_own = spread(
        jnp.concatenate(
            [
                w_in.reshape(rows, 2, chips, units).transpose(2, 0, 1, 3).reshape(chips, rows, -1),
                w_down.reshape(chips, units, rows).transpose(0, 2, 1),
            ],
            axis=2,
        )
    )
    in_own, down_own = ffn_own[:, : 2 * units], ffn_own[:, 2 * units :]
    out_own = lax.all_gather(w_out, "core", axis=0, tiled=True)

    def gather(value):
        return lax.all_gather(value, CHIPS, axis=0, tiled=True)

    def scatter(value):
        return lax.psum_scatter(value, CHIPS, scatter_dimension=0, tiled=True).astype(f32)

    normed_one, centered_one, inverse_one = layer_norm(x, gains[0])
    first = gather(normed_one.astype(bf16))
    top_all = gather(grad_top)
    tokens = first.shape[0]
    cos_np, sin_np = rope_tables(tokens)
    cos = take(jnp.asarray(cos_np), 0, core)
    sin = take(jnp.asarray(sin_np), 0, core)
    narrow = ((tokens, WIDE), bf16)
    part, q, k, v, att, lse = call(
        attend_kernel,
        [((tokens, features), bf16), narrow, narrow, narrow, narrow, ((tokens, 2), f32)],
        [],
        first, qkv_own, out_own, cos, sin,
    )
    residual = x + scatter(part)
    normed_two, centered_two, inverse_two = layer_norm(residual, gains[1])
    second = gather(normed_two.astype(bf16))
    upward = dot_nn(second, in_own)
    gated, gate_back = jax.vjp(gate_mix, upward)
    gated = gated.astype(bf16)
    grad_gated = dot_nn(top_all, down_own)
    grad_up = gate_back(grad_gated)[0].astype(bf16)
    grad_second = scatter(dot_nt(grad_up, in_own).astype(bf16))
    block_out = (residual + scatter(dot_nt(gated, down_own).astype(bf16))).astype(bf16)
    grad_norm_two, grad_gain_ffn = norm_back(grad_second, centered_two, inverse_two, gains[1])
    grad_resid = grad_top.astype(f32) + grad_norm_two
    branch = gather(grad_resid.astype(bf16))
    grad_ffn = jnp.concatenate(
        [dot_tn(second, grad_up).astype(bf16), dot_tn(top_all, gated).astype(bf16)], axis=1
    )

    def over_core(value):
        return take(value, 1, core).astype(f32) + swap_core(take(value, 1, 1 - core)).astype(f32)

    def over_replicas(value):
        if replicas == 2:
            return value.astype(f32) + lax.ppermute(value, "replica", [(0, 1), (1, 0)]).astype(f32)
        return lax.psum(value, "replica").astype(f32)

    def collect(value):
        halves = over_core(value.reshape(chips, 2, rows, value.shape[-1])).astype(bf16)
        return lax.all_to_all(halves, CHIPS, 0, 0, tiled=True)

    ffn_sum = over_replicas(collect(grad_ffn))
    grad_in = ffn_sum[:, :, : 2 * units].reshape(chips, rows, 2, units)
    grad_in = grad_in.transpose(1, 2, 0, 3).reshape(w_in.shape)
    grad_down = ffn_sum[:, :, 2 * units :].transpose(0, 2, 1).reshape(w_down.shape)

    part, grad_qkv, grad_out = call(
        attend_back_kernel,
        [((tokens, features), bf16), ((features, 3 * WIDE), bf16), ((WIDE, features), bf16)],
        [((tokens, 3 * WIDE), bf16), ((tokens, WIDE), f32), ((tokens, WIDE), f32)],
        branch, first, qkv_own, out_own, cos, sin, q, k, v, att, lse,
    )
    grad_first = scatter(part)
    grad_norm_one, grad_gain_attn = norm_back(grad_first, centered_one, inverse_one, gains[0])
    grad_hidden = (grad_resid + grad_norm_one).astype(bf16)
    grad_out = over_core(grad_out.reshape(1, 2, rows, features))[0].astype(bf16)
    grad_out = over_replicas(grad_out)

    qkv_sum = over_replicas(collect(grad_qkv))
    grad_qkv = qkv_sum.reshape(chips, rows, 3, WIDE).transpose(1, 2, 0, 3).reshape(w_qkv.shape)
    gain_parts = jnp.stack([grad_gain_attn, grad_gain_ffn])
    gain_sum = lax.psum(gain_parts, ("replica",) + CHIPS + ("core",))
    own = lax.axis_index(CHIPS + ("core",)) * rows
    gain_sum = lax.dynamic_slice_in_dim(gain_sum, own, rows, 1)

    done = jnp.stack([block_out, grad_hidden])
    back = swap_core(done[:, local_len:])
    mine = done[:, :local_len]
    pair = jnp.where(core == 0, jnp.stack([mine, back], 1), jnp.stack([back, mine], 1))
    return (pair[0], pair[1], grad_qkv, grad_out, grad_in, grad_down, gain_sum[0], gain_sum[1])


def solution(mesh):
    replicas, shards, ctx = (mesh.shape[name] for name in ("replica", "shard", "ctx"))
    fine = Mesh(
        mesh.devices.reshape(replicas, shards, ctx // 2, 2), ("replica", "shard", "cy", "core")
    )
    group = ("shard", "cy", "core")
    token = P("replica", group, None)
    row, col, vec = P(group, None), P(None, group), P(group)

    def body(*args):
        return on_device(replicas, shards * ctx // 2, *args)

    return jax.shard_map(
        body,
        mesh=fine,
        in_specs=(token, token, row, row, row, col, vec, vec),
        out_specs=(token, token, row, row, row, col, vec, vec),
        check_vma=False,
    )
```

time: 1070 us -> 643 us (0.60)
  waiting for transfers between devices: 744 us -> 343 us
  blocking collectives: 72 us -> 148 us
  matrix products: 86.5 us -> 20.2 us
  local copies, waits for them, and re-layouts: 94.9 us -> 47.9 us
  Pallas kernels: 0 us -> 27.8 us
  other arithmetic: 48.5 us -> 25.4 us
  starting transfers between devices: 0.73 us -> 13 us
    reduce_scatter x4, waiting for transfers between devices: 335 us -> 157 us  [scatter(): lax.psum_scatter(value, CHIPS, scatter_dimension=0, tiled=True).astype(f32)]
    unnamed x13 -> x9, waiting for transfers between devices: 157 us -> 0.15 us
    all_gather x6 -> x5, waiting for transfers between devices: 248 us -> 149 us  [the longest x4 149 us: gather(): return lax.all_gather(value, CHIPS, axis=0, tiled=True)]
    all_to_all x0 -> x2, blocking collectives: none -> 82.3 us  [the longest x1 44.8 us: collect(): return lax.all_to_all(halves, CHIPS, 0, 0, tiled=True)]
    unnamed x2 -> x0, blocking collectives: 67.1 us -> none
    dot_general x24 -> x6, matrix products: 86.5 us -> 20.2 us  [the longest x2 8.54 us: dot_nn(): lax.dot_general(a, b, (((1,), (0,)), ((), ())), preferred_element_type=f32)]
    psum x1, blocking collectives: 4.98 us -> 39 us  [on_device(): gain_sum = lax.psum(gain_parts, ('replica',) + CHIPS + ('core',))]
    slice x10 -> x2, local copies, waits for them, and re-layouts: 32.3 us -> 1.3 us  [the longest x1 1.29 us: on_device(): grad_in = ffn_sum[:, :, :2 * units].reshape(chips, rows, 2, units)]
  transfers between devices with their start and end apart: 12 -> 19, of which waited for: 12 -> 12; matrix products, arithmetic and copies ran while one was open for 11% -> 10% of each run, Pallas kernels for 0% -> 3%
where the time goes in v1:
time: 643 us; the launch traced here: 641 us
  waiting for transfers between devices  343 us (53%)
  blocking collectives  148 us (23%)
  local copies, waits for them, and re-layouts  47.9 us (7%)
  Pallas kernels  27.8 us (4%)
  other arithmetic  25.4 us (4%)
  matrix products  20.2 us (3%)
  between operations  16.2 us (3%)
  starting transfers between devices  13 us (2%)
    reduce_scatter x4, waiting for transfers between devices, scatter(): lax.psum_scatter(value, CHIPS, scatter_dimension=0, tiled=True).astype(f32)  157 us
    all_gather x4, waiting for transfers between devices, gather(): return lax.all_gather(value, CHIPS, axis=0, tiled=True)  149 us
    all_to_all x1, blocking collectives, collect(): return lax.all_to_all(halves, CHIPS, 0, 0, tiled=True)  44.8 us
    psum x1, blocking collectives, on_device(): gain_sum = lax.psum(gain_parts, ('replica',) + CHIPS + ('core',))  39 us
    all_to_all x1, blocking collectives, spread(): moved = lax.all_to_all(blocks, CHIPS, 0, 0, tiled=True)  37.4 us
    pallas_call x2, Pallas kernels, call(): pl.pallas_call(kernel, out_shape=[jax.ShapeDtypeStruct(s, d) for s, d in...  27.8 us
    all_gather x1, blocking collectives, on_device(): lax.all_gather(jnp.stack([norm_attn, norm_ffn]), CHIPS + ('core',), axis=...  22.6 us
    all_to_all x1, waiting for transfers between devices, spread(): moved = lax.all_to_all(blocks, CHIPS, 0, 0, tiled=True)  17.4 us
  transfers between devices with their start and end apart: 19, of which 12 were waited for; matrix products, arithmetic and copies ran while one was open for 10% of the time, Pallas kernels for 3%

profile of v1, /device:TPU:0, one launch (start us, length us, event | category | flops | bytes accessed | tf_op | source)
XLA Modules:
  0.0 641.3 jit_solution(14636083381550577857)
XLA Ops:
  8.1 1.8 dynamic-slice_bitcast_fusion.5
  10.5 22.6 %all-gather = bf16[16,64,2]{1,2,0:T(2,128)(2,1)S(1)} all-gather(bf16[1,64,2]{1,2,0:T(2,128)(2,1)S(1)} %maximum_bitcast_fusion), channel_id=1, replica_groups=mesh['replica'=2,'shard'=4,'cy'=2,'core'=2] {'shard','cy','core'}, dimensions={0}, use_global_device_ids=true | all-gather | bytes 4352 | tf_op jit(solution)/shard_map/all_gather | solution.py:181
  35.5 1.1 reshape.121
  36.5 3.5 all-to-all-start
  40.1 2.0 all_gather.27.w_out
  42.1 1.1 dynamic-slice_bitcast_fusion.1
  43.2 17.4 %all-to-all-done = bf16[8,64,384]{2,1,0:T(8,128)(2,1)S(1)} async-done(((bf16[8,64,384]{2,1,0:T(8,128)(2,1)}), bf16[8,64,384]{2,1,0:T(8,128)(2,1)S(1)}, u32[]{:S(2)}, u32[]{:S(2)}) %all-to-all-start) | async-done | bytes 393248 | tf_op jit(solution)/shard_map/all_to_all | solution.py:189
  60.5 2.4 all_gather.26
  62.9 25.3 %all-gather.7.cloned.1.call-done.first = bf16[1024,1024]{1,0:T(8,128)(2,1)} async-done(((bf16[128,1024]{1,0:T(8,128)(2,1)}), bf16[1024,1024]{1,0:T(8,128)(2,1)}) %all-gather.7.cloned.1.call-update) | async-done | bytes 2097168 | tf_op jit(solution)/shard_map/all_gather | solution.py:210
  88.2 10.6 %shard_map.161 = (bf16[1024,1024]{1,0:T(8,128)(2,1)S(1)}, bf16[1024,128]{1,0:T(8,128)(2,1)S(1)}, bf16[1024,128]{1,0:T(8,128)(2,1)S(1)}, bf16[1024,128]{1,0:T(8,1...) custom-call(bf16[1024,1024]{1,0:T(8,128)(2,1)} %all-gather.7.cloned.1.call-done.first, ...), custom_call_target="tpu_custom_call" | custom-call | tf_op jit(solution)/shard_map/pallas_call | solution.py:156
  98.8 1.4 copy-done
  102.4 1.5 reshape.125
  104.7 3.2 reshape.123
  107.9 2.7 copy.65
  110.6 3.0 reshape.124
  113.5 1.4 pad_maximum_fusion.1
  114.9 37.4 %all_to_all.20 = bf16[8,64,984]{2,1,0:T(8,128)(2,1)} all-to-all(bf16[8,64,984]{2,1,0:T(8,128)(2,1)S(1)} %pad_maximum_fusion.1), channel_id=1, replica_groups=mesh['replica'=2,'shard'=4,'cy'=2,'core'=2] {'shard','cy'}, dimensions={0} | all-to-all | bytes 2015232 | tf_op jit(solution)/shard_map/all_to_all | solution.py:189
  152.5 25.6 %reduce-scatter.5.cloned.1.call-done = bf16[128,1024]{1,0:T(8,128)(2,1)} async-done(((bf16[1024,1024]{1,0:T(8,128)(2,1)}), bf16[128,1024]{1,0:T(8,128)(2,1)}) %reduce-scatter.5.cloned.1.call-update) | async-done | bytes 262160 | tf_op jit(solution)/shard_map/reduce_scatter | solution.py:213
  178.1 1.1 fusion.39
  179.2 1.2 multiply_reduce_fusion
  180.3 1.8 multiply_convert_fusion.1
  183.2 47.2 %all-gather.9.cloned.1.call-done = bf16[1024,1024]{1,0:T(8,128)(2,1)} async-done(((bf16[128,1024]{1,0:T(8,128)(2,1)}), bf16[1024,1024]{1,0:T(8,128)(2,1)}) %all-gather.9.cloned.1.call-update) | async-done | bytes 2097168 | tf_op jit(solution)/shard_map/all_gather | solution.py:210
  230.5 3.7 fusion.2
  234.2 1.5 copy-done.18
  235.7 3.9 multiply_convert_fusion
  239.6 41.2 %all-gather.13.cloned.1.call-done = bf16[1024,1024]{1,0:T(8,128)(2,1)} async-done(((bf16[128,1024]{1,0:T(8,128)(2,1)}), bf16[1024,1024]{1,0:T(8,128)(2,1)}) %all-gather.13.cloned.1.call-update) | async-done | bytes 2097168 | tf_op jit(solution)/shard_map/all_gather | solution.py:210
  280.8 4.9 fusion.38
  285.7 1.1 copy-done.43
  287.2 3.2 convolution_convert_fusion.1
  290.4 4.2 convolution_convert_fusion
  294.7 62.0 %reduce-scatter.9.cloned.1.call-done = bf16[128,1024]{1,0:T(8,128)(2,1)} async-done(((bf16[1024,1024]{1,0:T(8,128)(2,1)}), bf16[128,1024]{1,0:T(8,128)(2,1)}) %reduce-scatter.9.cloned.1.call-update) | async-done | bytes 262160 | tf_op jit(solution)/shard_map/reduce_scatter | solution.py:213
  356.7 1.3 fusion.35
  358.1 69.0 %reduce-scatter.7.cloned.1.call-done = bf16[128,1024]{1,0:T(8,128)(2,1)} async-done(((bf16[1024,1024]{1,0:T(8,128)(2,1)}), bf16[128,1024]{1,0:T(8,128)(2,1)}) %reduce-scatter.7.cloned.1.call-update) | async-done | bytes 262160 | tf_op jit(solution)/shard_map/reduce_scatter | solution.py:213
  427.0 2.1 fusion.40
  429.4 2.7 convolution_convert_fusion.3
  432.6 1.6 convolution_convert_fusion.2
  434.2 1.5 pad_maximum_fusion
  435.7 3.9 copy.53
  439.6 2.3 dynamic-slice_bitcast_fusion
  441.9 35.6 %all-gather.15.cloned.1.call-done.branch = bf16[1024,1024]{1,0:T(8,128)(2,1)} async-done(((bf16[128,1024]{1,0:T(8,128)(2,1)}), bf16[1024,1024]{1,0:T(8,128)(2,1)}) %all-gather.15.cloned.1.call-update) | async-done | bytes 2097168 | tf_op jit(solution)/shard_map/all_gather | solution.py:210
  477.5 0.9 copy-done.2
  478.5 0.9 copy-done.4
  479.4 0.9 copy-done.6
  480.4 0.9 copy-done.8
  481.3 17.2 %shard_map.162 = (bf16[1024,1024]{1,0:T(8,128)(2,1)}, bf16[1024,384]{1,0:T(8,128)(2,1)S(1)}, bf16[128,1024]{1,0:T(8,128)(2,1)S(1)}) custom-call(bf16[1024,1024]{1,0:T(8,128)(2,1)} %all-gather.15.cloned.1.call-done.branch, bf16[1024,1024]{1,0:T(8,128)(2,1)} %all-gather.7.cloned.1.call-done.first, bf16[1024,384]{1,0:T(8,128)(2,1)S(1)} %bitcast.98, ...), custom_call_target="tpu_custom_call" | custom-call | tf_op jit(solution)/shard_map/pallas_call | solution.py:156
  499.3 1.6 copy-done.15
  500.8 1.6 fusion
  502.5 44.8 %all_to_all.21 = bf16[8,64,984]{2,1,0:T(8,128)(2,1)S(1)} all-to-all(bf16[8,64,984]{2,1,0:T(8,128)(2,1)S(1)} %fusion), channel_id=1, replica_groups=mesh['replica'=2,'shard'=4,'cy'=2,'core'=2] {'shard','cy'}, dimensions={0} | all-to-all | bytes 2015232 | tf_op jit(solution)/shard_map/all_to_all | solution.py:256
  547.3 1.5 collective-permute-start.7
  548.9 1.7 collective-permute-done.2
  551.4 4.4 all-to-all-start.2
  556.0 15.9 %collective-permute-done.7 = bf16[8,64,984]{2,1,0:T(8,128)(2,1)} collective-permute-done((bf16[8,64,984]{2,1,0:T(8,128)(2,1)S(1)}, bf16[8,64,984]{2,1,0:T(8,128)(2,1)}, u32[]{:S(2)}, u32[]{:S(2)}) %collective-permute-start.7) | collective-permute-done | bytes 1007648 | tf_op jit(solution)/shard_map/ppermute | solution.py:251
  571.9 1.9 convert_add_fusion.1
  573.9 1.5 collective-permute-start.5
  576.0 1.1 slice_bitcast_fusion
  577.2 1.3 slice.78
  578.4 2.6 reshape.132
  581.9 1.7 reshape.133
  584.1 1.1 reshape.134
  586.5 1.2 convert_add_fusion.3
  588.5 1.0 copy.64
  589.6 1.3 fusion.37
  590.9 39.0 %psum.7 = f32[2,1024]{1,0:T(2,128)S(1)} all-reduce(f32[2,1024]{1,0:T(2,128)S(1)} %pad_maximum_fusion.6), channel_id=1, replica_groups=mesh['replica'=2,'shard'=4,'cy'=2,'core'=2] {'replica','shard','cy','core'}, use_global_device_ids=true, to_apply=%region_14.15 | all-reduce | flops 2048 | bytes 16384 | tf_op jit(solution)/shard_map/psum | solution.py:278
  630.0 1.4 fusion.43
  (155 shorter events, 16.9 us)
Async XLA Ops:
  8.0 2.4 copy-start.41
  8.0 2.4 copy-start.42
  8.0 80.2 %all-gather.7.cloned.1.call-start = ((), (), s32[]{:S(2)}) async-start(), calls=%async_computation.8 | async-start | bytes 2359296 | tf_op jit(solution)/shard_map/all_gather | solution.py:210
  9.9 25.2 %copy-start.26 = (bf16[64,3072]{1,0:T(8,128)(2,1)S(1)}, bf16[64,3072]{1,0:T(8,128)(2,1)}, u32[]{:S(2)}) copy-start(bf16[64,3072]{1,0:T(8,128)(2,1)} %param.12) | copy-start | bytes 1179652
  9.9 23.2 %collective-permute-start = (bf16[2,64,1024]{2,1,0:T(8,128)(2,1)S(1)}, bf16[2,64,1024]{2,1,0:T(8,128)(2,1)S(1)}, u32[]{:S(2)}, u32[]{:S(2)}) collective-permute-start(bf16[2,64,1024]{2,1,0:T(8,128)(2,1)S(1)} %pad_maximum_fusion.3), channel_id=1, source_target_pairs={{0,1},{1,0},{2,3},{3,2},{4,5},{5,4},{6,7},{7,6},{8,9},{9,8},{10,11... | collective-permute-start | bytes 786440 | tf_op jit(solution)/shard_map/ppermute | solution.py:172
  33.8 393.2 %copy-start.11 = (bf16[64,1024]{1,0:T(8,128)(2,1)}, bf16[64,1024]{1,0:T(8,128)(2,1)S(1)}, u32[]{:S(2)}) copy-start(bf16[64,1024]{1,0:T(8,128)(2,1)S(1)} %get-tuple-element.45) | copy-start | bytes 393220
  33.9 1.3 copy-start.31
  34.2 1.0 copy-start.33
  35.2 4.8 copy-start.28
  35.2 6.8 %copy-start.27 = (f32[2,1024,128]{2,1,0:T(8,128)S(1)}, f32[2,1024,128]{2,1,0:T(8,128)}, u32[]{:S(2)}) copy-start(f32[2,1024,128]{2,1,0:T(8,128)} %constant.139.clone) | copy-start | bytes 3145732
  36.5 24.0 %all-to-all-start = ((bf16[8,64,384]{2,1,0:T(8,128)(2,1)}), bf16[8,64,384]{2,1,0:T(8,128)(2,1)S(1)}, u32[]{:S(2)}, u32[]{:S(2)}) async-start(bf16[8,64,384]{2,1,0:T(8,128)(2,1)} %reshape.121), calls=%async_computation | async-start | bytes 786432 | tf_op jit(solution)/shard_map/all_to_all | solution.py:189
  40.0 138.1 %reduce-scatter.5.cloned.1.call-start = ((), (), s32[]{:S(2)}) async-start(), calls=%async_computation.9 | async-start | bytes 2359296 | tf_op jit(solution)/shard_map/reduce_scatter | solution.py:213
  98.8 1.4 copy-start
  100.2 0.7 copy-start.1
  100.9 0.7 copy-start.3
  102.3 1.6 copy-start.7
  102.3 80.9 %all-gather.11.cloned.1.call-start = ((), (), s32[]{:S(2)}) async-start(), calls=%async_computation.11 | async-start | bytes 3145728 | tf_op jit(solution)/shard_map/all_gather | solution.py:190
  107.9 5.7 copy-start.24
  152.4 29.8 %copy-start.20 = (bf16[64,1024]{1,0:T(8,128)(2,1)S(1)}, bf16[64,1024]{1,0:T(8,128)(2,1)}, u32[]{:S(2)}) copy-start(bf16[64,1024]{1,0:T(8,128)(2,1)} %get-tuple-element.42) | copy-start | bytes 393220
  152.4 29.8 %copy-start.22 = (bf16[64,1024]{1,0:T(8,128)(2,1)S(1)}, bf16[64,1024]{1,0:T(8,128)(2,1)}, u32[]{:S(2)}) copy-start(bf16[64,1024]{1,0:T(8,128)(2,1)} %get-tuple-element.44) | copy-start | bytes 393220
  152.4 78.1 %all-gather.9.cloned.1.call-start = ((), (), s32[]{:S(2)}) async-start(), calls=%async_computation.10 | async-start | bytes 2359296 | tf_op jit(solution)/shard_map/all_gather | solution.py:210
  180.3 246.7 %copy-start.29 = (f32[128]{0:T(128)}, f32[128]{0:T(128)S(1)}, u32[]{:S(2)}) copy-start(f32[128]{0:T(128)S(1)} %add_rsqrt_fusion) | copy-start | bytes 1540
  182.2 98.6 %all-gather.13.cloned.1.call-start = ((), (), s32[]{:S(2)}) async-start(), calls=%async_computation.13 | async-start | bytes 2359296 | tf_op jit(solution)/shard_map/all_gather | solution.py:210
  183.0 173.8 %reduce-scatter.9.cloned.1.call-start = ((), (), s32[]{:S(2)}) async-start(), calls=%async_computation.14 | async-start | bytes 2359296 | tf_op jit(solution)/shard_map/reduce_scatter | solution.py:213
  234.1 1.6 copy-start.18
  280.8 6.4 copy-start.40
  285.7 1.1 copy-start.43
  285.7 1.5 copy-start.45
  290.4 136.6 %reduce-scatter.7.cloned.1.call-start = ((), (), s32[]{:S(2)}) async-start(), calls=%async_computation.12 | async-start | bytes 2359296 | tf_op jit(solution)/shard_map/reduce_scatter | solution.py:213
  294.6 62.1 %copy-start.13 = (bf16[128,1024]{1,0:T(8,128)(2,1)S(1)}, bf16[128,1024]{1,0:T(8,128)(2,1)}, u32[]{:S(2)}) copy-start(bf16[128,1024]{1,0:T(8,128)(2,1)} %reduce-scatter.5.cloned.1.call-done) | copy-start | bytes 786436
  294.6 182.9 %all-gather.15.cloned.1.call-start = ((), (), s32[]{:S(2)}) async-start(), calls=%async_computation.15 | async-start | bytes 2359296 | tf_op jit(solution)/shard_map/all_gather | solution.py:210
  358.0 71.1 %copy-start.35 = (f32[128]{0:T(128)}, f32[128]{0:T(128)S(1)}, u32[]{:S(2)}) copy-start(f32[128]{0:T(128)S(1)} %broadcast_multiply_fusion.2) | copy-start | bytes 1540
  358.0 71.1 %copy-start.37 = (f32[128]{0:T(128)}, f32[128]{0:T(128)S(1)}, u32[]{:S(2)}) copy-start(f32[128]{0:T(128)S(1)} %broadcast_multiply_fusion.3) | copy-start | bytes 1540
  429.1 160.4 %reduce-scatter.11.cloned.1.call-start = ((), (), s32[]{:S(2)}) async-start(), calls=%async_computation.16 | async-start | bytes 2359296 | tf_op jit(solution)/shard_map/reduce_scatter | solution.py:213
  429.4 2.8 copy-start.39
  429.4 2.8 copy-start.44
  429.4 3.2 copy-start.46
  441.9 57.4 %collective-permute-start.6 = (bf16[8,64,984]{2,1,0:T(8,128)(2,1)}, bf16[8,64,984]{2,1,0:T(8,128)(2,1)}, u32[]{:S(2)}, u32[]{:S(2)}) collective-permute-start(bf16[8,64,984]{2,1,0:T(8,128)(2,1)} %dynamic-slice_bitcast_fusion), channel_id=1, source_target_pairs={{0,1},{1,0},{2,3},{3,2},{4,5},{5,4},{6,7},{7,6},{8,9},{9,8},{10,11... | collective-permute-start | bytes 3022856 | tf_op jit(solution)/shard_map/ppermute | solution.py:172
  477.5 0.9 copy-start.2
  478.5 0.9 copy-start.4
  479.4 0.9 copy-start.6
  480.4 0.9 copy-start.8
  499.2 1.6 copy-start.15
  547.3 4.2 copy-start.16
  547.3 24.6 %collective-permute-start.7 = (bf16[8,64,984]{2,1,0:T(8,128)(2,1)S(1)}, bf16[8,64,984]{2,1,0:T(8,128)(2,1)}, u32[]{:S(2)}, u32[]{:S(2)}) collective-permute-start(bf16[8,64,984]{2,1,0:T(8,128)(2,1)S(1)} %all_to_all.21), channel_id=1, source_target_pairs={{0,16},{16,0},{1,17},{17,1},{2,18},{18,2},{3,19},{19,3},{4,20},{20... | collective-permute-start | bytes 3022856 | tf_op jit(solution)/shard_map/ppermute | solution.py:251
  548.7 7.1 %copy-start.10 = (bf16[128,1024]{1,0:T(8,128)(2,1)S(1)}, bf16[128,1024]{1,0:T(8,128)(2,1)}, u32[]{:S(2)}) copy-start(bf16[128,1024]{1,0:T(8,128)(2,1)} %copy-done.9) | copy-start | bytes 786436
  548.8 1.8 collective-permute-start.2
  551.4 24.0 %all-to-all-start.2 = ((bf16[8,64,384]{2,1,0:T(8,128)(2,1)}), bf16[8,64,384]{2,1,0:T(8,128)(2,1)}, u32[]{:S(2)}, u32[]{:S(2)}) async-start(bf16[8,64,384]{2,1,0:T(8,128)(2,1)} %fusion.11), calls=%async_computation.6 | async-start | bytes 786432 | tf_op jit(solution)/shard_map/all_to_all | solution.py:256
  555.8 18.0 %collective-permute-start.4 = (bf16[1,64,1024]{2,1,0:T(8,128)(2,1)S(1)}, bf16[1,64,1024]{2,1,0:T(8,128)(2,1)S(1)}, u32[]{:S(2)}, u32[]{:S(2)}) collective-permute-start(bf16[1,64,1024]{2,1,0:T(8,128)(2,1)S(1)} %dynamic-slice_bitcast_fusion.4), channel_id=1, source_target_pairs={{0,1},{1,0},{2,3},{3,2},{4,5},{5,4},{6,7},{7,6},{8,9},{9,8},{10,11... | collective-permute-start | bytes 393224 | tf_op jit(solution)/shard_map/ppermute | solution.py:172
  573.9 11.3 %collective-permute-start.5 = (bf16[64,1024]{1,0:T(8,128)(2,1)S(1)}, bf16[64,1024]{1,0:T(8,128)(2,1)S(1)}, u32[]{:S(2)}, u32[]{:S(2)}) collective-permute-start(bf16[64,1024]{1,0:T(8,128)(2,1)S(1)} %fusion.45), channel_id=1, source_target_pairs={{0,16},{16,0},{1,17},{17,1},{2,18},{18,2},{3,19},{19,3},{4,20},{20... | collective-permute-start | bytes 393224 | tf_op jit(solution)/shard_map/ppermute | solution.py:251
  575.4 11.0 %collective-permute-start.3 = (bf16[8,64,384]{2,1,0:T(8,128)(2,1)}, bf16[8,64,384]{2,1,0:T(8,128)(2,1)}, u32[]{:S(2)}, u32[]{:S(2)}) collective-permute-start(bf16[8,64,384]{2,1,0:T(8,128)(2,1)} %all-to-all-done.2), channel_id=1, source_target_pairs={{0,16},{16,0},{1,17},{17,1},{2,18},{18,2},{3,19},{19,3},{4,20},{20... | collective-permute-start | bytes 1179656 | tf_op jit(solution)/shard_map/ppermute | solution.py:251
  581.9 1.7 copy-start.17
  588.0 1.6 copy-start.12
  588.0 1.6 copy-start.32
  588.0 1.6 copy-start.34
  588.5 41.4 %copy-start.14 = (bf16[128,1024]{1,0:T(8,128)(2,1)S(1)}, bf16[128,1024]{1,0:T(8,128)(2,1)}, u32[]{:S(2)}) copy-start(bf16[128,1024]{1,0:T(8,128)(2,1)} %reduce-scatter.5.cloned.1.call-done) | copy-start | bytes 786436
  588.5 41.4 %copy-start.19 = (bf16[128,1024]{1,0:T(8,128)(2,1)S(1)}, bf16[128,1024]{1,0:T(8,128)(2,1)}, u32[]{:S(2)}) copy-start(bf16[128,1024]{1,0:T(8,128)(2,1)} %reduce-scatter.9.cloned.1.call-done) | copy-start | bytes 786436
  588.5 41.4 %copy-start.21 = (bf16[64,1024]{1,0:T(8,128)(2,1)S(1)}, bf16[64,1024]{1,0:T(8,128)(2,1)}, u32[]{:S(2)}) copy-start(bf16[64,1024]{1,0:T(8,128)(2,1)} %get-tuple-element.42) | copy-start | bytes 393220
  588.5 41.4 %copy-start.23 = (bf16[64,1024]{1,0:T(8,128)(2,1)S(1)}, bf16[64,1024]{1,0:T(8,128)(2,1)}, u32[]{:S(2)}) copy-start(bf16[64,1024]{1,0:T(8,128)(2,1)} %get-tuple-element.44) | copy-start | bytes 393220
  588.5 41.4 %copy-start.30 = (f32[128]{0:T(128)S(1)}, f32[128]{0:T(128)}, u32[]{:S(2)}) copy-start(f32[128]{0:T(128)} %copy-done.29) | copy-start | bytes 1540
  588.5 41.4 %copy-start.36 = (f32[128]{0:T(128)S(1)}, f32[128]{0:T(128)}, u32[]{:S(2)}) copy-start(f32[128]{0:T(128)} %copy-done.35) | copy-start | bytes 1540
  588.5 41.4 %copy-start.38 = (f32[128]{0:T(128)S(1)}, f32[128]{0:T(128)}, u32[]{:S(2)}) copy-start(f32[128]{0:T(128)} %copy-done.37) | copy-start | bytes 1540
  589.6 41.8 %copy-start.25 = (bf16[1,128,1024]{2,1,0:T(8,128)(2,1)S(1)}, bf16[1,128,1024]{2,1,0:T(8,128)(2,1)}, u32[]{:S(2)}) copy-start(bf16[1,128,1024]{2,1,0:T(8,128)(2,1)} %get-tuple-element.40) | copy-start | bytes 786436
  631.4 1.6 collective-permute-start.1
  (2 other events, 1.4 us)
Sparse Core Ops, SparseCore 0:
  35.2 52.9 all-gather.6
  102.4 75.5 reduce-scatter.4
  290.5 66.1 reduce-scatter.8
  360.1 66.8 reduce-scatter.6
Sparse Core Ops, SparseCore 1:
  152.5 9.7 all-gather.10
  182.2 48.2 all-gather.8
  233.1 47.7 all-gather.12
  429.2 48.3 all-gather.14
  499.4 80.1 reduce-scatter.10

commit v2 on v1

--- a/solution.py
+++ b/solution.py
@@ -163,6 +163,212 @@
     )(*args)
 
 
+def comm_kernel(shards, kinds, *refs):
+    count = len(kinds)
+    ins, outs, rest = refs[:count], refs[count : 2 * count], list(refs[2 * count :])
+    s, y, c = (lax.axis_index(name) for name in ("shard", "cy", "core"))
+    chips = 2 * shards
+    me = 2 * s + y
+    spreads = "spread" in kinds
+    barrier = pltpu.get_barrier_semaphore()
+    for step in range(1, chips):
+        peer = lax.rem(me + step, chips)
+        pl.semaphore_signal(barrier, inc=1, device_id=at_chip(peer // 2, lax.rem(peer, 2)), device_id_type=MESH)
+    if spreads:
+        pl.semaphore_signal(barrier, inc=1, device_id={"core": 1 - c}, device_id_type=MESH)
+    pl.semaphore_wait(barrier, chips if spreads else chips - 1)
+
+    def far(d):
+        return lax.rem(s + d, shards)
+
+    stages = [[], [], []]
+    for kind, src, dst in zip(kinds, ins, outs):
+        send, recv = rest.pop(0), rest.pop(0)
+        scratch = [rest.pop(0) for _ in range(2 if kind == "rs" else 0)]
+        for stage, step in zip(stages, MOVES[kind](src, dst, send, recv, scratch, shards, s, y, c, far)):
+            stage.append(step)
+    for stage in stages:
+        for step in stage:
+            step()
+
+
+MESH = pl.DeviceIdType.MESH
+
+
+def at_chip(shard, cy):
+    return {"shard": shard, "cy": cy}
+
+
+def remote(src, dst, send, recv, where):
+    return pltpu.make_async_remote_copy(
+        src_ref=src, dst_ref=dst, send_sem=send, recv_sem=recv, device_id=where, device_id_type=MESH
+    )
+
+
+def gather_moves(src, dst, send, recv, scratch, shards, s, y, c, far):
+    size = src.shape[0]
+
+    def place(shard, cy):
+        return dst.at[pl.ds(pl.multiple_of((2 * shard + cy) * size, size), size), :]
+
+    across = remote(src, place(s, y), send.at[0], recv.at[0], at_chip(s, 1 - y))
+    along = [
+        remote(src, place(s, y), send.at[d], recv.at[d], at_chip(far(d), y))
+        for d in range(1, shards)
+    ]
+    onward = []
+    for d in range(1, shards):
+        spot = place(far(shards - d), y)
+        slot = shards - 1 + d
+        onward.append(remote(spot, spot, send.at[slot], recv.at[slot], at_chip(s, 1 - y)))
+
+    def begin():
+        for copy in along:
+            copy.start()
+        across.start()
+        place(s, y)[...] = src[...]
+
+    def middle():
+        for first, second in zip(along, onward):
+            first.wait_recv()
+            second.start()
+
+    def finish():
+        for copy in along:
+            copy.wait_send()
+        across.wait()
+        for copy in onward:
+            copy.wait()
+
+    return begin, middle, finish
+
+
+def scatter_moves(src, dst, send, recv, scratch, shards, s, y, c, far):
+    size = dst.shape[0]
+    ybuf, zbuf = scratch
+
+    def part(shard, cy):
+        return src.at[pl.ds(pl.multiple_of((2 * shard + cy) * size, size), size), :]
+
+    order = list(range(1, shards)) + [0]
+    across = {
+        d: remote(part(far(d), 1 - y), ybuf.at[d], send.at[d], recv.at[d], at_chip(s, 1 - y))
+        for d in order
+    }
+    along = {
+        d: remote(
+            ybuf.at[shards + d], zbuf.at[d], send.at[shards + d], recv.at[shards + d],
+            at_chip(far(d), y),
+        )
+        for d in range(1, shards)
+    }
+
+    def begin():
+        for d in order:
+            across[d].start()
+
+    def middle():
+        for d in range(1, shards):
+            across[d].wait_recv()
+            ybuf[shards + d] = (part(far(d), y)[...].astype(f32) + ybuf[d].astype(f32)).astype(bf16)
+            along[d].start()
+
+    def finish():
+        across[0].wait_recv()
+        total = part(s, y)[...].astype(f32) + ybuf[0].astype(f32)
+        for d in range(1, shards):
+            along[d].wait_recv()
+            total = total + zbuf[d].astype(f32)
+        dst[...] = total
+        for d in order:
+            across[d].wait_send()
+        for d in range(1, shards):
+            along[d].wait_send()
+
+    return begin, middle, finish
+
+
+def swap_moves(src, dst, send, recv, scratch, shards, s, y, c, far, share=False):
+    chips, size = 2 * shards, src.shape[1]
+    me = 2 * s + y
+
+    def place(chip):
+        if share:
+            return dst.at[chip, pl.ds(pl.multiple_of(c * size, size), size), :]
+        return dst.at[chip]
+
+    out, onward = [], []
+    for e in range(1, chips):
+        peer = lax.rem(me + e, chips)
+        out.append(
+            remote(
+                src.at[peer], place(me), send.at[e], recv.at[e],
+                at_chip(peer // 2, lax.rem(peer, 2)),
+            )
+        )
+    for e in range(chips if share else 0):
+        spot = place(lax.rem(me + chips - e, chips))
+        first = src.at[me] if e == 0 else spot
+        onward.append(remote(first, spot, send.at[chips + e], recv.at[chips + e], {"core": 1 - c}))
+
+    def begin():
+        for copy in out:
+            copy.start()
+        if share:
+            onward[0].start()
+        place(me)[...] = src[me]
+
+    def middle():
+        for e in range(1, chips):
+            out[e - 1].wait_recv()
+            if share:
+                onward[e].start()
+
+    def finish():
+        for copy in out:
+            copy.wait_send()
+        for copy in onward:
+            copy.wait()
+
+    return begin, middle, finish
+
+
+def spread_moves(*args):
+    return swap_moves(*args, share=True)
+
+
+MOVES = {"ag": gather_moves, "rs": scatter_moves, "a2a": swap_moves, "spread": spread_moves}
+
+
+def exchange(shards, ident, *jobs):
+    chips = 2 * shards
+    outs, scratch = [], []
+    for kind, value in jobs:
+        shape, dtype = value.shape, value.dtype
+        slots = {"ag": chips, "rs": chips, "a2a": chips, "spread": 2 * chips}[kind]
+        scratch += [pltpu.SemaphoreType.DMA((slots,))] * 2
+        if kind == "ag":
+            shape = (chips * shape[0], shape[1])
+        elif kind == "rs":
+            shape, dtype = (shape[0] // chips, shape[1]), f32
+            scratch += [pltpu.VMEM((chips,) + shape, bf16), pltpu.VMEM((shards,) + shape, bf16)]
+        elif kind == "spread":
+            shape = (shape[0], 2 * shape[1], shape[2])
+        outs.append(jax.ShapeDtypeStruct(shape, dtype))
+    vmem = pl.BlockSpec(memory_space=pltpu.VMEM)
+    kinds = tuple(kind for kind, _ in jobs)
+    return pl.pallas_call(
+        lambda *refs: comm_kernel(shards, kinds, *refs),
+        out_shape=outs,
+        in_specs=[vmem] * len(jobs),
+        out_specs=[vmem] * len(jobs),
+        scratch_shapes=scratch,
+        compiler_params=pltpu.CompilerParams(
+            collective_id=ident, has_side_effects=True, vmem_limit_bytes=48 * 2**20
+        ),
+    )(*[value for _, value in jobs])
+
+
 def gate_mix(upward):
     half_width = upward.shape[1] // 2
     return jax.nn.gelu(upward[:, :half_width], approximate=False) * upward[:, half_width:]
@@ -172,48 +378,46 @@
     return lax.ppermute(value, "core", [(0, 1), (1, 0)])
 
 
-def on_device(replicas, chips, hidden, cotangent, w_qkv, w_out, w_in, w_down, norm_attn, norm_ffn):
+def on_device(replicas, shards, hidden, cotangent, w_qkv, w_out, w_in, w_down, norm_attn, norm_ffn):
     _, local_len, features = hidden.shape
+    chips = 2 * shards
     units = w_down.shape[0] // chips
     core = lax.axis_index("core")
     take = lambda value, axis, index: lax.dynamic_index_in_dim(value, index, axis, keepdims=False)
 
-    gains = lax.all_gather(
-        jnp.stack([norm_attn, norm_ffn]), CHIPS + ("core",), axis=1, tiled=True
-    ).astype(f32)
+    gain_pair = jnp.concatenate([norm_attn, norm_ffn])
+    gain_other = swap_core(gain_pair)
+    gain_rows = jnp.where(
+        core == 0, jnp.stack([gain_pair, gain_other]), jnp.stack([gain_other, gain_pair])
+    )
+    (gains,) = exchange(shards, 0, ("ag", jnp.pad(gain_rows, ((0, 14), (0, 0)))))
+    gains = gains.reshape(chips, 16, 2, -1)[:, :2].transpose(2, 0, 1, 3).reshape(2, features)
+    gains = gains.astype(f32)
     other = swap_core(jnp.stack([take(hidden, 0, 1 - core), take(cotangent, 0, 1 - core)]))
     x = jnp.concatenate([take(hidden, 0, core), other[0]]).astype(f32)
     grad_top = jnp.concatenate([take(cotangent, 0, core), other[1]])
 
-    def spread(blocks):
-        moved = lax.all_to_all(blocks, CHIPS, 0, 0, tiled=True)
-        both = lax.all_gather(moved, "core", axis=1, tiled=True)
-        return both.reshape(features, blocks.shape[-1])
-
     rows = w_qkv.shape[0]
-    qkv_own = spread(
+    qkv_blocks = (
         w_qkv.reshape(rows, 3, chips, WIDE).transpose(2, 0, 1, 3).reshape(chips, rows, 3 * WIDE)
     )
-    ffn_own = spread(
-        jnp.concatenate(
-            [
-                w_in.reshape(rows, 2, chips, units).transpose(2, 0, 1, 3).reshape(chips, rows, -1),
-                w_down.reshape(chips, units, rows).transpose(0, 2, 1),
-            ],
-            axis=2,
-        )
-    )
-    in_own, down_own = ffn_own[:, : 2 * units], ffn_own[:, 2 * units :]
+    ffn_blocks = jnp.concatenate(
+        [
+            w_in.reshape(rows, 2, chips, units).transpose(2, 0, 1, 3).reshape(chips, rows, -1),
+            w_down.reshape(chips, units, rows).transpose(0, 2, 1),
+        ],
+        axis=2,
+    )
     out_own = lax.all_gather(w_out, "core", axis=0, tiled=True)
 
     def gather(value):
         return lax.all_gather(value, CHIPS, axis=0, tiled=True)
 
-    def scatter(value):
-        return lax.psum_scatter(value, CHIPS, scatter_dimension=0, tiled=True).astype(f32)
-
     normed_one, centered_one, inverse_one = layer_norm(x, gains[0])
-    first = gather(normed_one.astype(bf16))
+    first, qkv_own = exchange(
+        shards, 1, ("ag", normed_one.astype(bf16)), ("spread", qkv_blocks)
+    )
+    qkv_own = qkv_own.reshape(features, 3 * WIDE)
     top_all = gather(grad_top)
     tokens = first.shape[0]
     cos_np, sin_np = rope_tables(tokens)
@@ -226,19 +430,27 @@
         [],
         first, qkv_own, out_own, cos, sin,
     )
-    residual = x + scatter(part)
+    attn_sum, ffn_own = exchange(shards, 2, ("rs", part), ("spread", ffn_blocks))
+    ffn_own = ffn_own.reshape(features, 3 * units)
+    in_own, down_own = ffn_own[:, : 2 * units], ffn_own[:, 2 * units :]
+    residual = x + attn_sum
     normed_two, centered_two, inverse_two = layer_norm(residual, gains[1])
-    second = gather(normed_two.astype(bf16))
+    (second,) = exchange(shards, 3, ("ag", normed_two.astype(bf16)))
     upward = dot_nn(second, in_own)
     gated, gate_back = jax.vjp(gate_mix, upward)
     gated = gated.astype(bf16)
     grad_gated = dot_nn(top_all, down_own)
     grad_up = gate_back(grad_gated)[0].astype(bf16)
-    grad_second = scatter(dot_nt(grad_up, in_own).astype(bf16))
-    block_out = (residual + scatter(dot_nt(gated, down_own).astype(bf16))).astype(bf16)
+    grad_second, down_sum = exchange(
+        shards,
+        4,
+        ("rs", dot_nt(grad_up, in_own).astype(bf16)),
+        ("rs", dot_nt(gated, down_own).astype(bf16)),
+    )
+    block_out = (residual + down_sum).astype(bf16)
     grad_norm_two, grad_gain_ffn = norm_back(grad_second, centered_two, inverse_two, gains[1])
     grad_resid = grad_top.astype(f32) + grad_norm_two
-    branch = gather(grad_resid.astype(bf16))
+    (branch,) = exchange(shards, 5, ("ag", grad_resid.astype(bf16)))
     grad_ffn = jnp.concatenate(
         [dot_tn(second, grad_up).astype(bf16), dot_tn(top_all, gated).astype(bf16)], axis=1
     )
@@ -251,14 +463,8 @@
             return value.astype(f32) + lax.ppermute(value, "replica", [(0, 1), (1, 0)]).astype(f32)
         return lax.psum(value, "replica").astype(f32)
 
-    def collect(value):
-        halves = over_core(value.reshape(chips, 2, rows, value.shape[-1])).astype(bf16)
-        return lax.all_to_all(halves, CHIPS, 0, 0, tiled=True)
-
-    ffn_sum = over_replicas(collect(grad_ffn))
-    grad_in = ffn_sum[:, :, : 2 * units].reshape(chips, rows, 2, units)
-    grad_in = grad_in.transpose(1, 2, 0, 3).reshape(w_in.shape)
-    grad_down = ffn_sum[:, :, 2 * units :].transpose(0, 2, 1).reshape(w_down.shape)
+    def halves(value):
+        return over_core(value.reshape(chips, 2, rows, value.shape[-1])).astype(bf16)
 
     part, grad_qkv, grad_out = call(
         attend_back_kernel,
@@ -266,18 +472,28 @@
         [((tokens, 3 * WIDE), bf16), ((tokens, WIDE), f32), ((tokens, WIDE), f32)],
         branch, first, qkv_own, out_own, cos, sin, q, k, v, att, lse,
     )
-    grad_first = scatter(part)
+    grad_first, ffn_sum, qkv_sum = exchange(
+        shards, 6, ("rs", part), ("a2a", halves(grad_ffn)), ("a2a", halves(grad_qkv))
+    )
+    ffn_sum = over_replicas(ffn_sum)
+    qkv_sum = over_replicas(qkv_sum)
+    grad_in = ffn_sum[:, :, : 2 * units].reshape(chips, rows, 2, units)
+    grad_in = grad_in.transpose(1, 2, 0, 3).reshape(w_in.shape)
+    grad_down = ffn_sum[:, :, 2 * units :].transpose(0, 2, 1).reshape(w_down.shape)
     grad_norm_one, grad_gain_attn = norm_back(grad_first, centered_one, inverse_one, gains[0])
     grad_hidden = (grad_resid + grad_norm_one).astype(bf16)
     grad_out = over_core(grad_out.reshape(1, 2, rows, features))[0].astype(bf16)
     grad_out = over_replicas(grad_out)
 
-    qkv_sum = over_replicas(collect(grad_qkv))
     grad_qkv = qkv_sum.reshape(chips, rows, 3, WIDE).transpose(1, 2, 0, 3).reshape(w_qkv.shape)
     gain_parts = jnp.stack([grad_gain_attn, grad_gain_ffn])
-    gain_sum = lax.psum(gain_parts, ("replica",) + CHIPS + ("core",))
-    own = lax.axis_index(CHIPS + ("core",)) * rows
-    gain_sum = lax.dynamic_slice_in_dim(gain_sum, own, rows, 1)
+    gain_parts = gain_parts.reshape(2, chips, 2, rows)
+    gain_half = take(gain_parts, 2, core) + swap_core(take(gain_parts, 2, 1 - core))
+    gain_half = gain_half.transpose(1, 0, 2).reshape(chips, 1, 2 * rows)
+    (gain_sum,) = exchange(
+        shards, 7, ("a2a", jnp.broadcast_to(gain_half, (chips, 8, 2 * rows)))
+    )
+    gain_sum = over_replicas(jnp.sum(gain_sum[:, 0], axis=0)).reshape(2, rows)
 
     done = jnp.stack([block_out, grad_hidden])
     back = swap_core(done[:, local_len:])
@@ -296,7 +512,7 @@
     row, col, vec = P(group, None), P(None, group), P(group)
 
     def body(*args):
-        return on_device(replicas, shards * ctx // 2, *args)
+        return on_device(replicas, shards, *args)
 
     return jax.shard_map(
         body,

time: 643 us -> 435 us (0.68)
  waiting for transfers between devices: 343 us -> 18.9 us
  Pallas kernels: 27.8 us -> 325 us
  blocking collectives: 148 us -> 2.07 us
  local copies, waits for them, and re-layouts: 47.9 us -> 31 us
  starting transfers between devices: 13 us -> 5.85 us
  matrix products: 20.2 us -> 13.6 us
    pallas_call x0 -> x8, Pallas kernels: none -> 297 us  [exchange(): pl.pallas_call(lambda *refs: comm_kernel(shards, kinds, *refs), out_shape...]
    reduce_scatter x4 -> x0, waiting for transfers between devices: 157 us -> none  [scatter(): lax.psum_scatter(value, CHIPS, scatter_dimension=0, tiled=True).astype(f32)]
    all_gather x4 -> x1, waiting for transfers between devices: 149 us -> 0.01 us  [gather(): return lax.all_gather(value, CHIPS, axis=0, tiled=True)]
    all_to_all x2 -> x0, blocking collectives: 82.3 us -> none  [the longest x1 44.8 us: collect(): return lax.all_to_all(halves, CHIPS, 0, 0, tiled=True)]
    psum x1 -> x0, blocking collectives: 39 us -> none  [on_device(): gain_sum = lax.psum(gain_parts, ('replica',) + CHIPS + ('core',))]
    all_gather x2 -> x0, blocking collectives: 24.9 us -> none  [the longest x1 22.6 us: on_device(): lax.all_gather(jnp.stack([norm_attn, norm_ffn]), CHIPS + ('core',), axis=...]
    all_to_all x2 -> x0, waiting for transfers between devices: 17.4 us -> none  [the longest x1 17.4 us: spread(): moved = lax.all_to_all(blocks, CHIPS, 0, 0, tiled=True)]
    all_to_all x2 -> x0, starting transfers between devices: 7.81 us -> none  [the longest x1 4.36 us: collect(): return lax.all_to_all(halves, CHIPS, 0, 0, tiled=True)]
  transfers between devices with their start and end apart: 19 -> 12, of which waited for: 12 -> 3; matrix products, arithmetic and copies ran while one was open for 10% -> 6% of each run, Pallas kernels for 3% -> 63%
where the time goes in v2:
time: 435 us; the launch traced here: 432 us
  Pallas kernels  325 us (75%)
  local copies, waits for them, and re-layouts  31 us (7%)
  other arithmetic  20.7 us (5%)
  waiting for transfers between devices  18.9 us (4%)
  between operations  14.9 us (3%)
  matrix products  13.6 us (3%)
  starting transfers between devices  5.85 us (1%)
    pallas_call x8, Pallas kernels, exchange(): pl.pallas_call(lambda *refs: comm_kernel(shards, kinds, *refs), out_shape...  297 us
    pallas_call x2, Pallas kernels, call(): pl.pallas_call(kernel, out_shape=[jax.ShapeDtypeStruct(s, d) for s, d in...  28 us
    ppermute x4, waiting for transfers between devices, over_replicas(): lax.ppermute(value, 'replica', [(0, 1), (1, 0)]).astype(f32)  17.6 us
  transfers between devices with their start and end apart: 12, of which 3 were waited for; matrix products, arithmetic and copies ran while one was open for 6% of the time, Pallas kernels for 63%

profile of v2, /device:TPU:0, one launch (start us, length us, event | category | flops | bytes accessed | tf_op | source)
XLA Modules:
  0.0 432.0 jit_solution(13108357532294208227)
XLA Ops:
  7.3 0.8 pad_maximum_fusion.6
  8.5 1.8 dynamic-slice_bitcast_fusion.5
  10.3 0.7 pad_maximum_fusion.3
  11.2 2.1 all_gather.6.w_out
  13.3 0.5 reshape.147
  13.9 1.4 reshape.145
  15.2 0.6 copy.58
  15.8 0.6 reshape.146
  16.8 0.9 copy-done.37
  18.1 0.9 copy-done.35
  19.7 10.5 %shard_map.161 = bf16[128,128]{1,0:T(8,128)(2,1)S(1)} custom-call(bf16[16,128]{1,0:T(8,128)(2,1)S(1)} %pad.10.refs_0_), custom_call_target="tpu_custom_call" | custom-call | tf_op jit(solution)/shard_map/pallas_call | solution.py:360
  30.3 1.0 slice_bitcast_fusion.3
  31.3 1.7 pad_maximum_fusion.5
  34.0 0.6 copy-done.45
  34.8 43.8 %shard_map.162 = (bf16[1024,1024]{1,0:T(8,128)(2,1)S(1)}, bf16[8,128,384]{2,1,0:T(8,128)(2,1)S(1)}) custom-call(bf16[128,1024]{1,0:T(8,128)(2,1)S(1)} %fusion.21.refs_0_, bf16[8,64,384]{2,1,0:T(8,128)(2,1)S(1)} %reshape.143.refs_1_), custom_call_target="tpu_custom_call" | custom-call | tf_op jit(solution)/shard_map/pallas_call | solution.py:360
  78.7 1.3 copy-done
  80.0 10.6 %shard_map.163 = (bf16[1024,1024]{1,0:T(8,128)(2,1)S(1)}, bf16[1024,128]{1,0:T(8,128)(2,1)S(1)}, bf16[1024,128]{1,0:T(8,128)(2,1)S(1)}, bf16[1024,128]{1,0:T(8,1...) custom-call(bf16[1024,1024]{1,0:T(8,128)(2,1)} %copy-done, bf16[1024,384]{1,0:T(8,128)(2,1)S(1)} %bitcast.91, ...), custom_call_target="tpu_custom_call" | custom-call | tf_op jit(solution)/shard_map/pallas_call | solution.py:156
  90.6 0.8 copy-done.6
  91.5 51.7 %shard_map.164 = (f32[128,1024]{1,0:T(8,128)S(1)}, bf16[8,128,984]{2,1,0:T(8,128)(2,1)S(1)}) custom-call(bf16[1024,1024]{1,0:T(8,128)(2,1)S(1)} %get-tuple-element.28.refs_0_, bf16[8,64,984]{2,1,0:T(8,128)(2,1)S(1)} %pad_maximum_fusion.1.refs_1_), custom_call_target="tpu_custom_call" | custom-call | tf_op jit(solution)/shard_map/pallas_call | solution.py:360
  143.7 33.5 %shard_map.165 = bf16[1024,1024]{1,0:T(8,128)(2,1)S(1)} custom-call(bf16[128,1024]{1,0:T(8,128)(2,1)S(1)} %multiply_convert_fusion.1.refs_0_), custom_call_target="tpu_custom_call" | custom-call | tf_op jit(solution)/shard_map/pallas_call | solution.py:360
  177.3 1.6 fusion.2
  178.9 3.8 multiply_convert_fusion
  182.8 2.8 convolution_convert_fusion.refs_1_
  185.5 4.9 %fusion.29 = (f32[1024,328]{0,1:T(8,128)S(1)}, f32[1024,328]{0,1:T(8,128)S(1)}) fusion(f32[1024,328]{0,1:T(8,128)} %get-tuple-element.55, f32[1024,656]{0,1:T(8,128)} %copy-done.26, bf16[1024,1024]{1,0:T(8,128)(2,1)} %all-gather.2.cloned.1.call-done, bf16[1024,984]{1,0:T(8,128)(2,1)} %bitcast.99), kind=kOutput, calls=%fused_computation.74 | convolution fusion | flops 693239808 | bytes 9601024 | tf_op jit(solution)/shard_map/dot_general | solution.py:38
  190.4 1.6 convolution_convert_fusion.2
  192.1 1.9 convolution_convert_fusion.1.refs_0_
  194.0 52.7 %shard_map.166 = (f32[128,1024]{1,0:T(8,128)S(1)}, f32[128,1024]{1,0:T(8,128)S(1)}) custom-call(bf16[1024,1024]{1,0:T(8,128)(2,1)S(1)} %convolution_convert_fusion.1.refs_0_, bf16[1024,1024]{1,0:T(8,128)(2,1)S(1)} %copy-done.5), custom_call_target="tpu_custom_call" | custom-call | tf_op jit(solution)/shard_map/pallas_call | solution.py:360
  246.7 0.9 multiply_reduce_fusion
  247.6 0.5 broadcast_multiply_fusion.2
  248.1 0.6 broadcast_multiply_fusion.3
  248.7 0.9 convolution_convert_fusion.3
  249.6 1.5 pad_maximum_fusion
  251.1 3.9 copy.42
  255.0 2.3 dynamic-slice_bitcast_fusion
  257.4 1.0 fusion.38
  258.4 36.7 %shard_map.167.branch = bf16[1024,1024]{1,0:T(8,128)(2,1)S(1)} custom-call(bf16[128,1024]{1,0:T(8,128)(2,1)S(1)} %get-tuple-element.52.refs_0_), custom_call_target="tpu_custom_call" | custom-call | tf_op jit(solution)/shard_map/pallas_call | solution.py:360
  295.2 1.4 copy-done.1
  296.6 17.4 %shard_map.168 = (bf16[1024,1024]{1,0:T(8,128)(2,1)}, bf16[1024,384]{1,0:T(8,128)(2,1)S(1)}, bf16[128,1024]{1,0:T(8,128)(2,1)S(1)}) custom-call(bf16[1024,1024]{1,0:T(8,128)(2,1)} %copy-done.1, bf16[1024,1024]{1,0:T(8,128)(2,1)} %copy-done, bf16[1024,384]{1,0:T(8,128)(2,1)S(1)} %bitcast.92, bf16[128,1024]{1,0:T(8,128)(2,1)S(1)} %all_gather.6.w_out, ...), custom_call_target="tpu_custom_call" | custom-call | tf_op jit(solution)/shard_map/pallas_call | solution.py:156
  314.0 0.8 dynamic-slice_bitcast_fusion.3
  314.8 0.6 collective-permute-start.6
  315.4 1.2 collective-permute-done.6
  316.7 1.7 collective-permute-start.7
  318.4 1.1 fusion.11.refs_2_
  319.5 1.8 fusion.refs_1_
  321.4 56.8 %shard_map.169 = (f32[128,1024]{1,0:T(8,128)S(1)}, bf16[8,64,984]{2,1,0:T(8,128)(2,1)S(1)}, bf16[8,64,384]{2,1,0:T(8,128)(2,1)S(1)}) custom-call(bf16[1024,1024]{1,0:T(8,128)(2,1)S(1)} %copy-done.2, bf16[8,64,984]{2,1,0:T(8,128)(2,1)S(1)} %fusion.refs_1_, bf16[8,64,384]{2,1,0:T(8,128)(2,1)S(1)} %fusion.11.refs_2_), custom_call_target="tpu_custom_call" | custom-call | tf_op jit(solution)/shard_map/pallas_call | solution.py:360
  378.5 0.5 broadcast_multiply_fusion
  379.1 0.5 broadcast_multiply_fusion.1
  379.8 0.9 fusion.33
  380.8 0.6 collective-permute-start.4
  381.8 11.2 %shard_map.170 = f32[8,8,128]{2,1,0:T(8,128)S(1)} custom-call(f32[8,8,128]{2,1,0:T(8,128)S(1)} %broadcast_in_dim.5.refs_0_), custom_call_target="tpu_custom_call" | custom-call | tf_op jit(solution)/shard_map/pallas_call | solution.py:360
  393.0 1.7 collective-permute-start.10
  394.7 0.7 convert_add_fusion.6
  395.8 11.6 %collective-permute-done.10 = f32[128]{0:T(128)S(1)} collective-permute-done((f32[128]{0:T(128)S(1)}, f32[128]{0:T(128)S(1)}, u32[]{:S(2)}, u32[]{:S(2)}) %collective-permute-start.10) | collective-permute-done | bytes 544 | tf_op jit(solution)/shard_map/ppermute | solution.py:463
  407.5 0.6 fusion.41
  408.1 0.8 slice_bitcast_fusion.1
  409.0 6.0 %collective-permute-done.5 = bf16[8,64,384]{2,1,0:T(8,128)(2,1)S(1)} collective-permute-done((bf16[8,64,384]{2,1,0:T(8,128)(2,1)S(1)}, bf16[8,64,384]{2,1,0:T(8,128)(2,1)S(1)}, u32[]{:S(2)}, u32[]{:S(2)}) %collective-permute-start.5) | collective-permute-done | bytes 393248 | tf_op jit(solution)/shard_map/ppermute | solution.py:463
  415.3 0.5 copy.45
  415.8 1.0 copy.57
  416.8 1.6 convert_add_fusion.1
  418.4 1.2 slice_bitcast_fusion
  419.7 1.2 reshape.154
  421.0 0.9 copy.46
  421.9 1.7 reshape.155
  424.0 1.1 reshape.156
  (160 shorter events, 6.5 us)
Async XLA Ops:
  7.2 3.9 copy-start.50
  7.2 3.9 copy-start.51
  7.2 4.0 copy-start.39
  7.2 6.1 %copy-start.36 = (bf16[2624,64]{0,1:T(8,128)(2,1)S(1)}, bf16[2624,64]{0,1:T(8,128)(2,1)}, u32[]{:S(2)}) copy-start(bf16[2624,64]{0,1:T(8,128)(2,1)} %param.15) | copy-start | bytes 1007620
  7.2 178.3 %all-gather.2.cloned.1.call-start = ((), (), s32[]{:S(2)}) async-start(), calls=%async_computation | async-start | bytes 2359296 | tf_op jit(solution)/shard_map/all_gather | solution.py:414
  8.1 11.6 %collective-permute-start.1 = (bf16[128]{0:T(256)(128)(2,1)S(1)}, bf16[128]{0:T(256)(128)(2,1)S(1)}, u32[]{:S(2)}, u32[]{:S(2)}) collective-permute-start(bf16[128]{0:T(256)(128)(2,1)S(1)} %pad_maximum_fusion.6), channel_id=1, source_target_pairs={{0,1},{1,0},{2,3},{3,2},{4,5},{5,4},{6,7},{7,6},{8,9},{9,8},{10,11... | collective-permute-start | bytes 776 | tf_op jit(solution)/shard_map/ppermute | solution.py:378
  10.3 23.3 %copy-start.20 = (bf16[64,1024]{1,0:T(8,128)(2,1)}, bf16[64,1024]{1,0:T(8,128)(2,1)S(1)}, u32[]{:S(2)}) copy-start(bf16[64,1024]{1,0:T(8,128)(2,1)S(1)} %get-tuple-element.78) | copy-start | bytes 393220
  10.3 3.5 copy-start.34
  11.1 19.3 %collective-permute-start = (bf16[2,64,1024]{2,1,0:T(8,128)(2,1)}, bf16[2,64,1024]{2,1,0:T(8,128)(2,1)}, u32[]{:S(2)}, u32[]{:S(2)}) collective-permute-start(bf16[2,64,1024]{2,1,0:T(8,128)(2,1)} %pad_maximum_fusion.3), channel_id=1, source_target_pairs={{0,1},{1,0},{2,3},{3,2},{4,5},{5,4},{6,7},{7,6},{8,9},{9,8},{10,11... | collective-permute-start | bytes 786440 | tf_op jit(solution)/shard_map/ppermute | solution.py:378
  16.5 1.2 copy-start.37
  16.5 1.5 copy-start.38
  18.0 1.0 copy-start.35
  31.3 2.3 copy-start.22
  31.3 2.3 copy-start.29
  33.4 0.6 copy-start.40
  34.0 0.6 copy-start.45
  78.6 1.4 copy-start
  90.6 0.8 copy-start.6
  91.4 51.7 %copy-start.8 = (bf16[1024,128]{1,0:T(8,128)(2,1)}, bf16[1024,128]{1,0:T(8,128)(2,1)S(1)}, u32[]{:S(2)}) copy-start(bf16[1024,128]{1,0:T(8,128)(2,1)S(1)} %get-tuple-element.34.k) | copy-start | bytes 786436
  91.4 51.7 %copy-start.10 = (bf16[1024,128]{1,0:T(8,128)(2,1)}, bf16[1024,128]{1,0:T(8,128)(2,1)S(1)}, u32[]{:S(2)}) copy-start(bf16[1024,128]{1,0:T(8,128)(2,1)S(1)} %get-tuple-element.35.v) | copy-start | bytes 786436
  91.4 51.8 %copy-start.12 = (bf16[1024,128]{1,0:T(8,128)(2,1)}, bf16[1024,128]{1,0:T(8,128)(2,1)S(1)}, u32[]{:S(2)}) copy-start(bf16[1024,128]{1,0:T(8,128)(2,1)S(1)} %get-tuple-element.36.att) | copy-start | bytes 786436
  91.4 51.8 %copy-start.21 = (bf16[64,1024]{1,0:T(8,128)(2,1)S(1)}, bf16[64,1024]{1,0:T(8,128)(2,1)}, u32[]{:S(2)}) copy-start(bf16[64,1024]{1,0:T(8,128)(2,1)} %copy-done.20) | copy-start | bytes 393220
  91.4 51.8 %copy-start.23 = (bf16[64,1024]{1,0:T(8,128)(2,1)S(1)}, bf16[64,1024]{1,0:T(8,128)(2,1)}, u32[]{:S(2)}) copy-start(bf16[64,1024]{1,0:T(8,128)(2,1)} %copy-done.22) | copy-start | bytes 393220
  143.2 39.6 %copy-start.14 = (bf16[8,128,984]{2,1,0:T(8,128)(2,1)}, bf16[8,128,984]{2,1,0:T(8,128)(2,1)S(1)}, u32[]{:S(2)}) copy-start(bf16[8,128,984]{2,1,0:T(8,128)(2,1)S(1)} %get-tuple-element.30) | copy-start | bytes 6045700
  143.4 33.9 %copy-start.16 = (f32[128,1024]{1,0:T(8,128)}, f32[128,1024]{1,0:T(8,128)S(1)}, u32[]{:S(2)}) copy-start(f32[128,1024]{1,0:T(8,128)S(1)} %get-tuple-element.57) | copy-start | bytes 1572868
  143.6 33.7 %copy-start.42 = (f32[128]{0:T(128)}, f32[128]{0:T(128)S(1)}, u32[]{:S(2)}) copy-start(f32[128]{0:T(128)S(1)} %add_rsqrt_fusion) | copy-start | bytes 1540
  177.3 1.6 copy-start.3
  178.9 3.8 copy-start.26
  182.8 2.8 copy-start.32
  185.5 4.9 %copy-start.4 = (bf16[1024,1024]{1,0:T(8,128)(2,1)S(1)}, bf16[1024,1024]{1,0:T(8,128)(2,1)}, u32[]{:S(2)}) copy-start(bf16[1024,1024]{1,0:T(8,128)(2,1)} %copy-done.3) | copy-start | bytes 6291460
  190.4 1.6 copy-start.15
  192.0 1.9 copy-start.5
  193.9 52.7 %copy-start.17 = (f32[128,1024]{1,0:T(8,128)S(1)}, f32[128,1024]{1,0:T(8,128)}, u32[]{:S(2)}) copy-start(f32[128,1024]{1,0:T(8,128)} %copy-done.16) | copy-start | bytes 1572868
  193.9 52.7 %copy-start.43 = (f32[128]{0:T(128)S(1)}, f32[128]{0:T(128)}, u32[]{:S(2)}) copy-start(f32[128]{0:T(128)} %copy-done.42) | copy-start | bytes 1540
  194.0 54.7 %copy-start.49 = (bf16[1024,1024]{1,0:T(8,128)(2,1)S(1)}, bf16[1024,1024]{1,0:T(8,128)(2,1)}, u32[]{:S(2)}) copy-start(bf16[1024,1024]{1,0:T(8,128)(2,1)} %all-gather.2.cloned.1.call-done) | copy-start | bytes 6291460
  246.7 2.0 copy-start.33
  255.0 2.4 copy-start.18
  255.0 2.4 copy-start.28
  255.0 2.4 copy-start.30
  255.0 2.4 copy-start.44
  255.0 2.4 copy-start.47
  255.0 2.4 copy-start.48
  257.3 62.2 %collective-permute-start.2 = (bf16[8,64,984]{2,1,0:T(8,128)(2,1)}, bf16[8,64,984]{2,1,0:T(8,128)(2,1)}, u32[]{:S(2)}, u32[]{:S(2)}) collective-permute-start(bf16[8,64,984]{2,1,0:T(8,128)(2,1)} %dynamic-slice_bitcast_fusion), channel_id=1, source_target_pairs={{0,1},{1,0},{2,3},{3,2},{4,5},{5,4},{6,7},{7,6},{8,9},{9,8},{10,11... | collective-permute-start | bytes 3022856 | tf_op jit(solution)/shard_map/ppermute | solution.py:378
  258.4 38.1 %copy-start.7 = (f32[1024,2]{1,0:T(8,128)S(1)}, f32[1024,2]{1,0:T(8,128)}, u32[]{:S(2)}) copy-start(f32[1024,2]{1,0:T(8,128)} %copy-done.6) | copy-start | bytes 24580
  258.4 38.1 %copy-start.9 = (bf16[1024,128]{1,0:T(8,128)(2,1)S(1)}, bf16[1024,128]{1,0:T(8,128)(2,1)}, u32[]{:S(2)}) copy-start(bf16[1024,128]{1,0:T(8,128)(2,1)} %copy-done.8) | copy-start | bytes 786436
  258.4 38.1 %copy-start.11 = (bf16[1024,128]{1,0:T(8,128)(2,1)S(1)}, bf16[1024,128]{1,0:T(8,128)(2,1)}, u32[]{:S(2)}) copy-start(bf16[1024,128]{1,0:T(8,128)(2,1)} %copy-done.10) | copy-start | bytes 786436
  258.4 38.1 %copy-start.13 = (bf16[1024,128]{1,0:T(8,128)(2,1)S(1)}, bf16[1024,128]{1,0:T(8,128)(2,1)}, u32[]{:S(2)}) copy-start(bf16[1024,128]{1,0:T(8,128)(2,1)} %copy-done.12) | copy-start | bytes 786436
  295.1 1.4 copy-start.1
  314.0 5.6 %copy-start.19 = (bf16[1024,984]{1,0:T(8,128)(2,1)S(1)}, bf16[1024,984]{1,0:T(8,128)(2,1)}, u32[]{:S(2)}) copy-start(bf16[1024,984]{1,0:T(8,128)(2,1)} %copy.42) | copy-start | bytes 6045700
  314.8 3.6 collective-permute-start.3
  314.8 1.9 collective-permute-start.6
  316.7 78.0 %collective-permute-start.7 = (bf16[64,1024]{1,0:T(8,128)(2,1)S(1)}, bf16[64,1024]{1,0:T(8,128)(2,1)S(1)}, u32[]{:S(2)}, u32[]{:S(2)}) collective-permute-start(bf16[64,1024]{1,0:T(8,128)(2,1)S(1)} %fusion.35), channel_id=1, source_target_pairs={{0,16},{16,0},{1,17},{17,1},{2,18},{18,2},{3,19},{19,3},{4,20},{20... | collective-permute-start | bytes 393224 | tf_op jit(solution)/shard_map/ppermute | solution.py:463
  319.5 1.9 copy-start.2
  321.4 56.8 %copy-start.24 = (bf16[64,1024]{1,0:T(8,128)(2,1)S(1)}, bf16[64,1024]{1,0:T(8,128)(2,1)}, u32[]{:S(2)}) copy-start(bf16[64,1024]{1,0:T(8,128)(2,1)} %copy-done.22) | copy-start | bytes 393220
  321.4 56.8 %copy-start.41 = (f32[128]{0:T(128)S(1)}, f32[128]{0:T(128)}, u32[]{:S(2)}) copy-start(f32[128]{0:T(128)} %copy-done.40) | copy-start | bytes 1540
  321.4 56.8 %copy-start.46 = (f32[128]{0:T(128)S(1)}, f32[128]{0:T(128)}, u32[]{:S(2)}) copy-start(f32[128]{0:T(128)} %copy-done.45) | copy-start | bytes 1540
  321.4 58.3 %copy-start.27 = (f32[128,1024]{1,0:T(8,128)S(1)}, f32[128,1024]{1,0:T(8,128)}, u32[]{:S(2)}) copy-start(f32[128,1024]{1,0:T(8,128)} %get-tuple-element.53) | copy-start | bytes 1572868
  378.2 2.5 copy-start.31
  379.7 2.0 collective-permute-start.9
  380.8 27.3 %collective-permute-start.4 = (bf16[2,64,1024]{2,1,0:T(8,128)(2,1)S(1)}, bf16[2,64,1024]{2,1,0:T(8,128)(2,1)S(1)}, u32[]{:S(2)}, u32[]{:S(2)}) collective-permute-start(bf16[2,64,1024]{2,1,0:T(8,128)(2,1)S(1)} %get-tuple-element.63), channel_id=1, source_target_pairs={{0,1},{1,0},{2,3},{3,2},{4,5},{5,4},{6,7},{7,6},{8,9},{9,8},{10,11... | collective-permute-start | bytes 786440 | tf_op jit(solution)/shard_map/ppermute | solution.py:378
  381.3 35.5 %collective-permute-start.8 = (bf16[8,64,984]{2,1,0:T(8,128)(2,1)S(1)}, bf16[8,64,984]{2,1,0:T(8,128)(2,1)}, u32[]{:S(2)}, u32[]{:S(2)}) collective-permute-start(bf16[8,64,984]{2,1,0:T(8,128)(2,1)S(1)} %get-tuple-element.43), channel_id=1, source_target_pairs={{0,16},{16,0},{1,17},{17,1},{2,18},{18,2},{3,19},{19,3},{4,20},{20... | collective-permute-start | bytes 3022856 | tf_op jit(solution)/shard_map/ppermute | solution.py:463
  393.0 14.4 %collective-permute-start.10 = (f32[128]{0:T(128)S(1)}, f32[128]{0:T(128)S(1)}, u32[]{:S(2)}, u32[]{:S(2)}) collective-permute-start(f32[128]{0:T(128)S(1)} %slice_reduce_fusion.2), channel_id=1, source_target_pairs={{0,16},{16,0},{1,17},{17,1},{2,18},{18,2},{3,19},{19,3},{4,20},{20... | collective-permute-start | bytes 1544 | tf_op jit(solution)/shard_map/ppermute | solution.py:463
  395.4 19.5 %collective-permute-start.5 = (bf16[8,64,384]{2,1,0:T(8,128)(2,1)S(1)}, bf16[8,64,384]{2,1,0:T(8,128)(2,1)S(1)}, u32[]{:S(2)}, u32[]{:S(2)}) collective-permute-start(bf16[8,64,384]{2,1,0:T(8,128)(2,1)S(1)} %get-tuple-element.41), channel_id=1, source_target_pairs={{0,16},{16,0},{1,17},{17,1},{2,18},{18,2},{3,19},{19,3},{4,20},{20... | collective-permute-start | bytes 1179656 | tf_op jit(solution)/shard_map/ppermute | solution.py:463
  421.9 1.7 copy-start.25
Sparse Core Ops, SparseCore 0:
  33.2 70.0 all-gather.1

commit v3 on v2

--- a/solution.py
+++ b/solution.py
@@ -74,7 +74,7 @@
     return jnp.where(lane < HEAD_DIM, first, second)
 
 
-def attend_kernel(first, w_qkv, w_out, cos, sin, part, q, k, v, att, lse):
+def attend_kernel(visit, first, w_qkv, w_out, cos, sin, part, q, k, v, att, lse):
     tokens = first.shape[0]
 
     @pl.loop(0, tokens // BLOCK)
@@ -87,9 +87,9 @@
         k[rows, :] = (pk * c + swap_halves(pk) * s).astype(bf16)
         v[rows, :] = packed[:, 2 * WIDE :].astype(bf16)
 
-    @pl.loop(0, tokens // BLOCK)
-    def _(i):
-        rows = pl.ds(pl.multiple_of(i * BLOCK, BLOCK), BLOCK)
+    size = tokens // len(visit)
+    for i, sent in visit:
+        rows = pl.ds(pl.multiple_of(i * size, size), size)
         q_rows = q[rows, :]
         outs = []
         for head in range(2):
@@ -103,10 +103,11 @@
         joined = join_heads(*outs).astype(bf16)
         att[rows, :] = joined
         part[rows, :] = dot_nn(joined, w_out[...]).astype(bf16)
+        sent.start()
 
 
 def attend_back_kernel(
-    branch, first, w_qkv, w_out, cos, sin, q, k, v, att, lse,
+    visit, between, branch, first, w_qkv, w_out, cos, sin, q, k, v, att, lse,
     part, grad_qkv, grad_out, dpacked, dk, dv,
 ):
     tokens = branch.shape[0]
@@ -134,14 +135,16 @@
         dq = dq * cos[rows, :] - swap_halves(dq) * sin[rows, :]
         dpacked[rows, :WIDE] = dq.astype(bf16)
 
-    @pl.loop(0, tokens // BLOCK)
-    def _(i):
-        rows = pl.ds(pl.multiple_of(i * BLOCK, BLOCK), BLOCK)
+    between()
+    size = tokens // len(visit)
+    for i, sent in visit:
+        rows = pl.ds(pl.multiple_of(i * size, size), size)
         d = dk[rows, :] * HEAD_DIM**-0.5
         d = d * cos[rows, :] - swap_halves(d) * sin[rows, :]
         dpacked[rows, WIDE : 2 * WIDE] = d.astype(bf16)
         dpacked[rows, 2 * WIDE :] = dv[rows, :].astype(bf16)
         part[rows, :] = dot_nt(dpacked[rows, :], w_qkv[...]).astype(bf16)
+        sent.start()
 
     grad_out[...] = dot_tn(att[...], branch[...]).astype(bf16)
 
@@ -151,41 +154,104 @@
         grad_qkv[cols, :] = dot_tn(first[:, cols], dpacked[...]).astype(bf16)
 
 
-def call(kernel, outs, scratch, *args):
+def call(kernel, ident, outs, scratch, *args):
     vmem = pl.BlockSpec(memory_space=pltpu.VMEM)
     return pl.pallas_call(
         kernel,
         out_shape=[jax.ShapeDtypeStruct(s, d) for s, d in outs],
         in_specs=[vmem] * len(args),
         out_specs=[vmem] * len(outs),
-        scratch_shapes=[pltpu.VMEM(s, d) for s, d in scratch],
-        compiler_params=pltpu.CompilerParams(vmem_limit_bytes=48 * 2**20),
+        scratch_shapes=[pltpu.VMEM(*x) if isinstance(x, tuple) else x for x in scratch],
+        compiler_params=pltpu.CompilerParams(
+            collective_id=ident, has_side_effects=True, vmem_limit_bytes=48 * 2**20
+        ),
     )(*args)
+
+
+def visits(far, across, shards):
+    return [(far(d), across[d]) for d in list(range(1, shards)) + [0]]
+
+
+def attend_send_kernel(
+    shards, first, w_qkv, w_out, cos, sin, ffn_blocks,
+    attn_sum, ffn_own, q, k, v, att, lse, part, send1, recv1, ybuf, zbuf, send2, recv2,
+):
+    env = greet(shards, True)
+    spread = spread_moves(ffn_blocks, ffn_own, send2, recv2, [], shards, *env)
+    scatter = scatter_moves(part, attn_sum, send1, recv1, [ybuf, zbuf], shards, *env)
+    spread[0]()
+    attend_kernel(
+        visits(env[3], scatter[3], shards),
+        first, w_qkv, w_out, cos, sin, part, q, k, v, att, lse,
+    )
+    scatter[1]()
+    spread[1]()
+    scatter[2]()
+    spread[2]()
+
+
+def attend_back_send_kernel(
+    shards, branch, first, w_qkv, w_out, cos, sin, q, k, v, att, lse, down_part, ffn_halves,
+    grad_first, down_sum, ffn_sum, grad_qkv, grad_out, part, dpacked, dk, dv,
+    send1, recv1, ybuf1, zbuf1, send2, recv2, ybuf2, zbuf2, send3, recv3,
+):
+    env = greet(shards, False)
+    scatter = scatter_moves(part, grad_first, send1, recv1, [ybuf1, zbuf1], shards, *env)
+    down = scatter_moves(down_part, down_sum, send2, recv2, [ybuf2, zbuf2], shards, *env)
+    swap = swap_moves(ffn_halves, ffn_sum, send3, recv3, [], shards, *env)
+    down[0]()
+    swap[0]()
+    attend_back_kernel(
+        visits(env[3], scatter[3], shards), down[1],
+        branch, first, w_qkv, w_out, cos, sin, q, k, v, att, lse,
+        part, grad_qkv, grad_out, dpacked, dk, dv,
+    )
+    scatter[1]()
+    down[2]()
+    swap[1]()
+    scatter[2]()
+    swap[2]()
+
+
+def sems(count):
+    return [pltpu.SemaphoreType.DMA((count,))] * 2
+
+
+def scatter_scratch(shards, rows, features):
+    return sems(2 * shards) + [
+        ((2 * shards, rows, features), bf16), ((shards, rows, features), bf16)
+    ]
+
+
+def greet(shards, spreads):
+    s, y, c = (lax.axis_index(name) for name in ("shard", "cy", "core"))
+    chips = 2 * shards
+    me = 2 * s + y
+    barrier = pltpu.get_barrier_semaphore()
+    for step in range(1, chips):
+        peer = lax.rem(me + step, chips)
+        pl.semaphore_signal(
+            barrier, inc=1, device_id=at_chip(peer // 2, lax.rem(peer, 2)), device_id_type=MESH
+        )
+    if spreads:
+        pl.semaphore_signal(barrier, inc=1, device_id={"core": 1 - c}, device_id_type=MESH)
+    pl.semaphore_wait(barrier, chips if spreads else chips - 1)
+
+    def far(d):
+        return lax.rem(s + d, shards)
+
+    return s, y, c, far
 
 
 def comm_kernel(shards, kinds, *refs):
     count = len(kinds)
     ins, outs, rest = refs[:count], refs[count : 2 * count], list(refs[2 * count :])
-    s, y, c = (lax.axis_index(name) for name in ("shard", "cy", "core"))
-    chips = 2 * shards
-    me = 2 * s + y
-    spreads = "spread" in kinds
-    barrier = pltpu.get_barrier_semaphore()
-    for step in range(1, chips):
-        peer = lax.rem(me + step, chips)
-        pl.semaphore_signal(barrier, inc=1, device_id=at_chip(peer // 2, lax.rem(peer, 2)), device_id_type=MESH)
-    if spreads:
-        pl.semaphore_signal(barrier, inc=1, device_id={"core": 1 - c}, device_id_type=MESH)
-    pl.semaphore_wait(barrier, chips if spreads else chips - 1)
-
-    def far(d):
-        return lax.rem(s + d, shards)
-
+    env = greet(shards, "spread" in kinds)
     stages = [[], [], []]
     for kind, src, dst in zip(kinds, ins, outs):
         send, recv = rest.pop(0), rest.pop(0)
         scratch = [rest.pop(0) for _ in range(2 if kind == "rs" else 0)]
-        for stage, step in zip(stages, MOVES[kind](src, dst, send, recv, scratch, shards, s, y, c, far)):
+        for stage, step in zip(stages, MOVES[kind](src, dst, send, recv, scratch, shards, *env)):
             stage.append(step)
     for stage in stages:
         for step in stage:
@@ -207,25 +273,34 @@
 
 def gather_moves(src, dst, send, recv, scratch, shards, s, y, c, far):
     size = src.shape[0]
-
-    def place(shard, cy):
-        return dst.at[pl.ds(pl.multiple_of((2 * shard + cy) * size, size), size), :]
+    cuts = 4 if size % 64 == 0 else 1
+    step = size // cuts
+
+    def place(shard, cy, cut=0, rows=size):
+        start = pl.multiple_of((2 * shard + cy) * size + cut * step, step)
+        return dst.at[pl.ds(start, rows), :]
 
     across = remote(src, place(s, y), send.at[0], recv.at[0], at_chip(s, 1 - y))
-    along = [
-        remote(src, place(s, y), send.at[d], recv.at[d], at_chip(far(d), y))
-        for d in range(1, shards)
-    ]
-    onward = []
-    for d in range(1, shards):
-        spot = place(far(shards - d), y)
-        slot = shards - 1 + d
-        onward.append(remote(spot, spot, send.at[slot], recv.at[slot], at_chip(s, 1 - y)))
+    along, onward = [], []
+    for cut in range(cuts):
+        for d in range(1, shards):
+            slot = 1 + cut * 2 * shards + d
+            along.append(
+                remote(
+                    src.at[pl.ds(cut * step, step), :], place(s, y, cut, step),
+                    send.at[slot], recv.at[slot], at_chip(far(d), y),
+                )
+            )
+            spot = place(far(shards - d), y, cut, step)
+            slot += shards
+            onward.append(remote(spot, spot, send.at[slot], recv.at[slot], at_chip(s, 1 - y)))
 
     def begin():
-        for copy in along:
+        for copy in along[: shards - 1]:
             copy.start()
         across.start()
+        for copy in along[shards - 1 :]:
+            copy.start()
         place(s, y)[...] = src[...]
 
     def middle():
@@ -285,7 +360,7 @@
         for d in range(1, shards):
             along[d].wait_send()
 
-    return begin, middle, finish
+    return begin, middle, finish, across
 
 
 def swap_moves(src, dst, send, recv, scratch, shards, s, y, c, far, share=False):
@@ -345,7 +420,7 @@
     outs, scratch = [], []
     for kind, value in jobs:
         shape, dtype = value.shape, value.dtype
-        slots = {"ag": chips, "rs": chips, "a2a": chips, "spread": 2 * chips}[kind]
+        slots = {"ag": 4 * chips + 1, "rs": chips, "a2a": chips, "spread": 2 * chips}[kind]
         scratch += [pltpu.SemaphoreType.DMA((slots,))] * 2
         if kind == "ag":
             shape = (chips * shape[0], shape[1])
@@ -424,13 +499,19 @@
     cos = take(jnp.asarray(cos_np), 0, core)
     sin = take(jnp.asarray(sin_np), 0, core)
     narrow = ((tokens, WIDE), bf16)
-    part, q, k, v, att, lse = call(
-        attend_kernel,
-        [((tokens, features), bf16), narrow, narrow, narrow, narrow, ((tokens, 2), f32)],
-        [],
-        first, qkv_own, out_own, cos, sin,
-    )
-    attn_sum, ffn_own = exchange(shards, 2, ("rs", part), ("spread", ffn_blocks))
+    own_rows = x.shape[0]
+    attn_sum, ffn_own, q, k, v, att, lse = call(
+        lambda *refs: attend_send_kernel(shards, *refs),
+        2,
+        [
+            ((own_rows, features), f32), ((chips, 2 * rows, 3 * units), bf16),
+            narrow, narrow, narrow, narrow, ((tokens, 2), f32),
+        ],
+        [((tokens, features), bf16)]
+        + scatter_scratch(shards, own_rows, features)
+        + sems(2 * chips),
+        first, qkv_own, out_own, cos, sin, ffn_blocks,
+    )
     ffn_own = ffn_own.reshape(features, 3 * units)
     in_own, down_own = ffn_own[:, : 2 * units], ffn_own[:, 2 * units :]
     residual = x + attn_sum
@@ -441,13 +522,8 @@
     gated = gated.astype(bf16)
     grad_gated = dot_nn(top_all, down_own)
     grad_up = gate_back(grad_gated)[0].astype(bf16)
-    grad_second, down_sum = exchange(
-        shards,
-        4,
-        ("rs", dot_nt(grad_up, in_own).astype(bf16)),
-        ("rs", dot_nt(gated, down_own).astype(bf16)),
-    )
-    block_out = (residual + down_sum).astype(bf16)
+    down_part = dot_nt(gated, down_own).astype(bf16)
+    (grad_second,) = exchange(shards, 4, ("rs", dot_nt(grad_up, in_own).astype(bf16)))
     grad_norm_two, grad_gain_ffn = norm_back(grad_second, centered_two, inverse_two, gains[1])
     grad_resid = grad_top.astype(f32) + grad_norm_two
     (branch,) = exchange(shards, 5, ("ag", grad_resid.astype(bf16)))
@@ -466,17 +542,25 @@
     def halves(value):
         return over_core(value.reshape(chips, 2, rows, value.shape[-1])).astype(bf16)
 
-    part, grad_qkv, grad_out = call(
-        attend_back_kernel,
-        [((tokens, features), bf16), ((features, 3 * WIDE), bf16), ((WIDE, features), bf16)],
-        [((tokens, 3 * WIDE), bf16), ((tokens, WIDE), f32), ((tokens, WIDE), f32)],
+    grad_first, down_sum, ffn_sum, grad_qkv, grad_out = call(
+        lambda *refs: attend_back_send_kernel(shards, *refs),
+        6,
+        [
+            ((own_rows, features), f32), ((own_rows, features), f32),
+            ((chips, rows, 3 * units), bf16),
+            ((features, 3 * WIDE), bf16), ((WIDE, features), bf16),
+        ],
+        [
+            ((tokens, features), bf16), ((tokens, 3 * WIDE), bf16),
+            ((tokens, WIDE), f32), ((tokens, WIDE), f32),
+        ]
+        + scatter_scratch(shards, own_rows, features) * 2
+        + sems(chips),
         branch, first, qkv_own, out_own, cos, sin, q, k, v, att, lse,
-    )
-    grad_first, ffn_sum, qkv_sum = exchange(
-        shards, 6, ("rs", part), ("a2a", halves(grad_ffn)), ("a2a", halves(grad_qkv))
-    )
+        down_part, halves(grad_ffn),
+    )
+    block_out = (residual + down_sum).astype(bf16)
     ffn_sum = over_replicas(ffn_sum)
-    qkv_sum = over_replicas(qkv_sum)
     grad_in = ffn_sum[:, :, : 2 * units].reshape(chips, rows, 2, units)
     grad_in = grad_in.transpose(1, 2, 0, 3).reshape(w_in.shape)
     grad_down = ffn_sum[:, :, 2 * units :].transpose(0, 2, 1).reshape(w_down.shape)
@@ -485,16 +569,17 @@
     grad_out = over_core(grad_out.reshape(1, 2, rows, features))[0].astype(bf16)
     grad_out = over_replicas(grad_out)
 
-    grad_qkv = qkv_sum.reshape(chips, rows, 3, WIDE).transpose(1, 2, 0, 3).reshape(w_qkv.shape)
     gain_parts = jnp.stack([grad_gain_attn, grad_gain_ffn])
     gain_parts = gain_parts.reshape(2, chips, 2, rows)
     gain_half = take(gain_parts, 2, core) + swap_core(take(gain_parts, 2, 1 - core))
     gain_half = gain_half.transpose(1, 0, 2).reshape(chips, 1, 2 * rows)
-    (gain_sum,) = exchange(
-        shards, 7, ("a2a", jnp.broadcast_to(gain_half, (chips, 8, 2 * rows)))
+    qkv_sum, gain_sum = exchange(
+        shards, 7, ("a2a", halves(grad_qkv)), ("a2a", jnp.broadcast_to(gain_half, (chips, 8, 2 * rows)))
     )
     gain_sum = over_replicas(jnp.sum(gain_sum[:, 0], axis=0)).reshape(2, rows)
 
+    qkv_sum = over_replicas(qkv_sum)
+    grad_qkv = qkv_sum.reshape(chips, rows, 3, WIDE).transpose(1, 2, 0, 3).reshape(w_qkv.shape)
     done = jnp.stack([block_out, grad_hidden])
     back = swap_core(done[:, local_len:])
     mine = done[:, :local_len]

time: 435 us -> 420 us (0.966)
  Pallas kernels: 325 us -> 308 us
  waiting for transfers between devices: 18.9 us -> 13.2 us
    pallas_call x8 -> x6, Pallas kernels: 297 us -> 187 us  [exchange(): pl.pallas_call(lambda *refs: comm_kernel(shards, kinds, *refs), out_shape...]
    pallas_call x2, Pallas kernels: 28 us -> 121 us  [call(): pl.pallas_call(kernel, out_shape=[jax.ShapeDtypeStruct(s, d) for s, d in...]
    ppermute x4, waiting for transfers between devices: 17.6 us -> 13.1 us  [over_replicas(): lax.ppermute(value, 'replica', [(0, 1), (1, 0)]).astype(f32)]
  transfers between devices with their start and end apart: 12 -> 12, of which waited for: 3 -> 2; matrix products, arithmetic and copies ran while one was open for 6% -> 7% of each run, Pallas kernels for 63% -> 58%
where the time goes in v3:
time: 420 us; the launch traced here: 413 us
  Pallas kernels  308 us (73%)
  local copies, waits for them, and re-layouts  34.1 us (8%)
  other arithmetic  19.4 us (5%)
  between operations  15.4 us (4%)
  matrix products  15.3 us (4%)
  waiting for transfers between devices  13.2 us (3%)
  starting transfers between devices  6 us (1%)
    pallas_call x6, Pallas kernels, exchange(): pl.pallas_call(lambda *refs: comm_kernel(shards, kinds, *refs), out_shape...  187 us
    pallas_call x2, Pallas kernels, call(): pl.pallas_call(kernel, out_shape=[jax.ShapeDtypeStruct(s, d) for s, d in...  121 us
    ppermute x4, waiting for transfers between devices, over_replicas(): lax.ppermute(value, 'replica', [(0, 1), (1, 0)]).astype(f32)  13.1 us
    unnamed x107, local copies, waits for them, and re-layouts  9.15 us
  transfers between devices with their start and end apart: 12, of which 2 were waited for; matrix products, arithmetic and copies ran while one was open for 7% of the time, Pallas kernels for 58%

profile of v3, /device:TPU:0, one launch (start us, length us, event | category | flops | bytes accessed | tf_op | source)
XLA Modules:
  0.0 413.4 jit_solution(2137940678038563534)
XLA Ops:
  7.3 0.8 pad_maximum_fusion.6
  8.1 0.5 collective-permute-start.1
  8.5 1.0 dynamic-slice_bitcast_fusion.6
  9.5 1.0 dynamic-slice_bitcast_fusion.5
  10.5 0.7 pad_maximum_fusion.3
  11.4 2.1 all_gather.6.refs_2_.refs_3_
  13.5 0.5 reshape.147
  14.0 0.8 copy.60
  14.8 1.3 reshape.145
  16.1 0.6 copy.58
  16.7 0.6 reshape.146
  17.4 1.4 pad_maximum_fusion.1.refs_5_
  19.1 0.9 copy-done.32
  20.3 1.1 reshape.143.refs_1_
  21.4 11.0 %shard_map.161 = bf16[128,128]{1,0:T(8,128)(2,1)S(1)} custom-call(bf16[16,128]{1,0:T(8,128)(2,1)S(1)} %pad.10.refs_0_), custom_call_target="tpu_custom_call" | custom-call | tf_op jit(solution)/shard_map/pallas_call | solution.py:435
  32.5 1.0 slice_bitcast_fusion.3
  33.5 0.8 pad_maximum_fusion.5
  35.3 0.5 copy-done.42
  36.0 1.0 copy-done.6
  37.0 52.0 %shard_map.162 = (bf16[1024,1024]{1,0:T(8,128)(2,1)S(1)}, bf16[8,128,384]{2,1,0:T(8,128)(2,1)S(1)}) custom-call(bf16[128,1024]{1,0:T(8,128)(2,1)S(1)} %fusion.21.refs_0_, bf16[8,64,384]{2,1,0:T(8,128)(2,1)S(1)} %copy-done.6), custom_call_target="tpu_custom_call" | custom-call | tf_op jit(solution)/shard_map/pallas_call | solution.py:435
  89.0 1.4 copy-done
  90.4 51.1 %shard_map.163 = (f32[128,1024]{1,0:T(8,128)S(1)}, bf16[8,128,984]{2,1,0:T(8,128)(2,1)}, bf16[1024,128]{1,0:T(8,128)(2,1)S(1)}, bf16[1024,128]{1,0:T(8,128)(2,1)...) custom-call(bf16[1024,1024]{1,0:T(8,128)(2,1)} %copy-done, ...), custom_call_target="tpu_custom_call" | custom-call | tf_op jit(solution)/shard_map/pallas_call | solution.py:159
  141.9 0.4 copy-done.7
  142.7 38.4 %shard_map.164 = bf16[1024,1024]{1,0:T(8,128)(2,1)S(1)} custom-call(bf16[128,1024]{1,0:T(8,128)(2,1)S(1)} %multiply_convert_fusion.1.refs_0_), custom_call_target="tpu_custom_call" | custom-call | tf_op jit(solution)/shard_map/pallas_call | solution.py:435
  181.1 1.6 fusion.2
  182.8 4.0 multiply_convert_fusion
  186.8 0.8 copy-done.29
  187.6 2.8 convolution_convert_fusion.refs_11_
  190.4 4.9 %fusion.29 = (f32[1024,328]{0,1:T(8,128)S(1)}, f32[1024,328]{0,1:T(8,128)S(1)}) fusion(f32[1024,328]{0,1:T(8,128)} %get-tuple-element.49, f32[1024,656]{0,1:T(8,128)} %copy-done.25, bf16[1024,1024]{1,0:T(8,128)(2,1)} %all-gather.2.cloned.1.call-done, bf16[1024,984]{1,0:T(8,128)(2,1)} %bitcast.112), kind=kOutput, calls=%fused_computation.74 | convolution fusion | flops 693239808 | bytes 9601024 | tf_op jit(solution)/shard_map/dot_general | solution.py:38
  195.4 1.6 convolution_convert_fusion.2
  197.0 1.1 copy-done.45
  198.1 0.9 convolution_convert_fusion.3
  199.0 1.5 pad_maximum_fusion
  200.5 3.9 copy.42
  204.4 2.5 dynamic-slice_bitcast_fusion
  206.8 3.6 convolution_convert_fusion.1.refs_0_
  210.5 36.8 %shard_map.165 = f32[128,1024]{1,0:T(8,128)S(1)} custom-call(bf16[1024,1024]{1,0:T(8,128)(2,1)S(1)} %convolution_convert_fusion.1.refs_0_), custom_call_target="tpu_custom_call" | custom-call | tf_op jit(solution)/shard_map/pallas_call | solution.py:435
  247.6 1.7 fusion.39
  249.4 31.8 %shard_map.166.refs_0_ = bf16[1024,1024]{1,0:T(8,128)(2,1)S(1)} custom-call(bf16[128,1024]{1,0:T(8,128)(2,1)S(1)} %get-tuple-element.50.refs_0_), custom_call_target="tpu_custom_call" | custom-call | tf_op jit(solution)/shard_map/pallas_call | solution.py:435
  281.2 3.4 fusion.refs_12_
  284.8 70.2 %shard_map.167 = (f32[128,1024]{1,0:T(8,128)S(1)}, f32[128,1024]{1,0:T(8,128)S(1)}, bf16[8,64,984]{2,1,0:T(8,128)(2,1)}, bf16[1024,384]{1,0:T(8,128)(2,1)S(1)}, bf16[128,1024]{1,0:T(8,128)(2,1)S(1)}) custom-call(bf16[1024,1024]{1,0:T(8,128)(2,1)} %copy-done.1, bf16[1024,1024]{1,0:T(8,128)(2,1)} %copy-done, bf16[1024,384]{1,0:T(8,128)(2,1)S(1)} %bitcast.92, ...), custom_call_target="tpu_custom_call" | custom-call | tf_op jit(solution)/shard_map/pallas_call | solution.py:159
  355.1 0.6 copy-done.17
  356.5 0.9 dynamic-slice_bitcast_fusion.4
  357.4 0.6 collective-permute-start.7
  358.4 0.5 collective-permute-start.4
  358.9 1.5 collective-permute-start.9
  360.6 0.6 collective-permute-start.8
  361.3 0.8 slice_bitcast_fusion.1
  362.2 16.8 %shard_map.168 = (bf16[8,64,384]{2,1,0:T(8,128)(2,1)S(1)}, f32[8,8,128]{2,1,0:T(8,128)S(1)}) custom-call(bf16[8,64,384]{2,1,0:T(8,128)(2,1)S(1)} %fusion.11.refs_0_, f32[8,8,128]{2,1,0:T(8,128)S(1)} %broadcast_in_dim.5.refs_1_), custom_call_target="tpu_custom_call" | custom-call | tf_op jit(solution)/shard_map/pallas_call | solution.py:435
  379.0 1.6 collective-permute-start.10
  380.6 0.5 collective-permute-start.6
  381.1 6.9 %collective-permute-done.8 = bf16[64,1024]{1,0:T(8,128)(2,1)S(1)} collective-permute-done((bf16[64,1024]{1,0:T(8,128)(2,1)S(1)}, bf16[64,1024]{1,0:T(8,128)(2,1)S(1)}, u32[]{:S(2)}, u32[]{:S(2)}) %collective-permute-start.8) | collective-permute-done | bytes 131104 | tf_op jit(solution)/shard_map/ppermute | solution.py:539
  388.0 0.7 convert_add_fusion.6
  388.7 0.6 fusion.41
  389.3 6.2 %collective-permute-done.6 = bf16[8,64,384]{2,1,0:T(8,128)(2,1)S(1)} collective-permute-done((bf16[8,64,384]{2,1,0:T(8,128)(2,1)S(1)}, bf16[8,64,384]{2,1,0:T(8,128)(2,1)S(1)}, u32[]{:S(2)}, u32[]{:S(2)}) %collective-permute-start.6) | collective-permute-done | bytes 393248 | tf_op jit(solution)/shard_map/ppermute | solution.py:539
  395.9 0.5 copy.46
  396.4 1.0 copy.57
  397.4 1.9 convert_add_fusion.1
  399.4 1.2 slice_bitcast_fusion
  400.7 1.2 reshape.154
  401.9 0.9 copy.47
  402.8 1.7 reshape.155
  404.5 0.5 copy.48
  405.0 1.1 reshape.156
  (160 shorter events, 5.4 us)
Async XLA Ops:
  7.2 4.1 %copy-start.48 = (bf16[64]{0:T(256)(128)(2,1)S(1)}, bf16[64]{0:T(256)(128)(2,1)}, u32[]{:S(2)}) copy-start(bf16[64]{0:T(256)(128)(2,1)} %param.17) | copy-start | bytes 388
  7.2 4.1 %copy-start.49 = (bf16[64]{0:T(256)(128)(2,1)S(1)}, bf16[64]{0:T(256)(128)(2,1)}, u32[]{:S(2)}) copy-start(bf16[64]{0:T(256)(128)(2,1)} %param.16) | copy-start | bytes 388
  7.2 4.2 %copy-start.36 = (bf16[64,1024]{1,0:T(8,128)(2,1)S(1)}, bf16[64,1024]{1,0:T(8,128)(2,1)}, u32[]{:S(2)}) copy-start(bf16[64,1024]{1,0:T(8,128)(2,1)} %param.13) | copy-start | bytes 393220
  7.2 6.3 %copy-start.33 = (bf16[2624,64]{0,1:T(8,128)(2,1)S(1)}, bf16[2624,64]{0,1:T(8,128)(2,1)}, u32[]{:S(2)}) copy-start(bf16[2624,64]{0,1:T(8,128)(2,1)} %param.15) | copy-start | bytes 1007620
  7.2 183.2 %all-gather.2.cloned.1.call-start = ((), (), s32[]{:S(2)}) async-start(), calls=%async_computation | async-start | bytes 2359296 | tf_op jit(solution)/shard_map/all_gather | solution.py:489
  8.1 13.3 %collective-permute-start.1 = (bf16[128]{0:T(256)(128)(2,1)S(1)}, bf16[128]{0:T(256)(128)(2,1)S(1)}, u32[]{:S(2)}, u32[]{:S(2)}) collective-permute-start(bf16[128]{0:T(256)(128)(2,1)S(1)} %pad_maximum_fusion.6), channel_id=1, source_target_pairs={{0,1},{1,0},{2,3},{3,2},{4,5},{5,4},{6,7},{7,6},{8,9},{9,8},{10,11... | collective-permute-start | bytes 776 | tf_op jit(solution)/shard_map/ppermute | solution.py:453
  10.5 4.3 %copy-start.31 = (bf16[64,5248]{1,0:T(8,128)(2,1)S(1)}, bf16[64,5248]{1,0:T(8,128)(2,1)}, u32[]{:S(2)}) copy-start(bf16[64,5248]{1,0:T(8,128)(2,1)} %param.14) | copy-start | bytes 2015236
  11.2 21.3 %collective-permute-start = (bf16[2,64,1024]{2,1,0:T(8,128)(2,1)}, bf16[2,64,1024]{2,1,0:T(8,128)(2,1)}, u32[]{:S(2)}, u32[]{:S(2)}) collective-permute-start(bf16[2,64,1024]{2,1,0:T(8,128)(2,1)} %pad_maximum_fusion.3), channel_id=1, source_target_pairs={{0,1},{1,0},{2,3},{3,2},{4,5},{5,4},{6,7},{7,6},{8,9},{9,8},{10,11... | collective-permute-start | bytes 786440 | tf_op jit(solution)/shard_map/ppermute | solution.py:453
  13.5 76.9 %copy-start.2 = (bf16[128,1024]{1,0:T(8,128)(2,1)}, bf16[128,1024]{1,0:T(8,128)(2,1)S(1)}, u32[]{:S(2)}) copy-start(bf16[128,1024]{1,0:T(8,128)(2,1)S(1)} %all_gather.6.refs_2_.refs_3_) | copy-start | bytes 786436
  17.4 1.4 copy-start.34
  17.4 1.7 copy-start.35
  19.0 1.0 copy-start.32
  33.5 1.4 copy-start.27
  33.5 108.0 %copy-start.22 = (bf16[64,1024]{1,0:T(8,128)(2,1)}, bf16[64,1024]{1,0:T(8,128)(2,1)S(1)}, u32[]{:S(2)}) copy-start(bf16[64,1024]{1,0:T(8,128)(2,1)S(1)} %get-tuple-element.63) | copy-start | bytes 393220
  34.7 0.6 copy-start.37
  35.3 0.5 copy-start.42
  36.0 1.0 copy-start.6
  89.0 1.4 copy-start
  141.5 0.8 copy-start.7
  141.5 0.9 copy-start.11
  141.5 1.0 copy-start.13
  141.5 1.0 copy-start.15
  141.5 39.6 %copy-start.9 = (bf16[1024,128]{1,0:T(8,128)(2,1)}, bf16[1024,128]{1,0:T(8,128)(2,1)S(1)}, u32[]{:S(2)}) copy-start(bf16[1024,128]{1,0:T(8,128)(2,1)S(1)} %get-tuple-element.28.refs_6_) | copy-start | bytes 786436
  141.7 105.9 %copy-start.19 = (f32[128,1024]{1,0:T(8,128)}, f32[128,1024]{1,0:T(8,128)S(1)}, u32[]{:S(2)}) copy-start(f32[128,1024]{1,0:T(8,128)S(1)} %get-tuple-element.53) | copy-start | bytes 1572868
  141.7 105.5 %copy-start.40 = (f32[128]{0:T(128)}, f32[128]{0:T(128)S(1)}, u32[]{:S(2)}) copy-start(f32[128]{0:T(128)S(1)} %broadcast_multiply_fusion.4) | copy-start | bytes 1540
  142.6 104.7 %copy-start.41 = (f32[128]{0:T(128)}, f32[128]{0:T(128)S(1)}, u32[]{:S(2)}) copy-start(f32[128]{0:T(128)S(1)} %add_rsqrt_fusion) | copy-start | bytes 1540
  142.7 38.4 %copy-start.46 = (bf16[8,128,984]{2,1,0:T(8,128)(2,1)S(1)}, bf16[8,128,984]{2,1,0:T(8,128)(2,1)}, u32[]{:S(2)}) copy-start(bf16[8,128,984]{2,1,0:T(8,128)(2,1)} %get-tuple-element.27) | copy-start | bytes 6045700
  181.1 1.6 copy-start.4
  182.8 4.0 copy-start.25
  186.8 0.8 copy-start.29
  190.4 4.9 %copy-start.5 = (bf16[1024,1024]{1,0:T(8,128)(2,1)S(1)}, bf16[1024,1024]{1,0:T(8,128)(2,1)}, u32[]{:S(2)}) copy-start(bf16[1024,1024]{1,0:T(8,128)(2,1)} %copy-done.4) | copy-start | bytes 6291460
  195.3 1.6 copy-start.50
  195.3 1.6 copy-start.51
  195.4 1.6 copy-start.30
  195.4 2.7 copy-start.45
  204.4 2.5 copy-start.47
  206.8 74.4 %collective-permute-start.2 = (bf16[8,64,984]{2,1,0:T(8,128)(2,1)}, bf16[8,64,984]{2,1,0:T(8,128)(2,1)}, u32[]{:S(2)}, u32[]{:S(2)}) collective-permute-start(bf16[8,64,984]{2,1,0:T(8,128)(2,1)} %dynamic-slice_bitcast_fusion), channel_id=1, source_target_pairs={{0,1},{1,0},{2,3},{3,2},{4,5},{5,4},{6,7},{7,6},{8,9},{9,8},{10,11... | collective-permute-start | bytes 3022856 | tf_op jit(solution)/shard_map/ppermute | solution.py:453
  210.4 37.2 %copy-start.28 = (bf16[64,1024]{1,0:T(8,128)(2,1)S(1)}, bf16[64,1024]{1,0:T(8,128)(2,1)}, u32[]{:S(2)}) copy-start(bf16[64,1024]{1,0:T(8,128)(2,1)} %copy-done.27) | copy-start | bytes 393220
  249.4 31.9 %copy-start.21 = (bf16[1024,984]{1,0:T(8,128)(2,1)S(1)}, bf16[1024,984]{1,0:T(8,128)(2,1)}, u32[]{:S(2)}) copy-start(bf16[1024,984]{1,0:T(8,128)(2,1)} %copy.42) | copy-start | bytes 6045700
  281.1 3.5 copy-start.1
  281.1 3.5 copy-start.3
  281.2 3.5 copy-start.8
  281.2 3.5 copy-start.10
  281.2 3.5 copy-start.12
  281.2 3.5 copy-start.14
  281.2 3.5 copy-start.16
  284.7 70.3 %copy-start.20 = (f32[128,1024]{1,0:T(8,128)S(1)}, f32[128,1024]{1,0:T(8,128)}, u32[]{:S(2)}) copy-start(f32[128,1024]{1,0:T(8,128)} %copy-done.19) | copy-start | bytes 1572868
  284.7 70.9 %copy-start.38 = (f32[128]{0:T(128)S(1)}, f32[128]{0:T(128)}, u32[]{:S(2)}) copy-start(f32[128]{0:T(128)} %copy-done.37) | copy-start | bytes 1540
  284.7 70.9 %copy-start.43 = (f32[128]{0:T(128)S(1)}, f32[128]{0:T(128)}, u32[]{:S(2)}) copy-start(f32[128]{0:T(128)} %copy-done.42) | copy-start | bytes 1540
  355.0 0.7 copy-start.17
  355.0 1.0 copy-start.23
  355.0 2.9 copy-start.26
  355.0 2.9 copy-start.39
  355.0 2.9 copy-start.44
  356.4 4.1 collective-permute-start.5
  357.4 3.2 collective-permute-start.7
  358.2 2.4 copy-start.18
  358.2 2.9 collective-permute-start.3
  358.4 3.7 collective-permute-start.4
  358.9 38.5 %collective-permute-start.9 = (bf16[8,64,984]{2,1,0:T(8,128)(2,1)}, bf16[8,64,984]{2,1,0:T(8,128)(2,1)}, u32[]{:S(2)}, u32[]{:S(2)}) collective-permute-start(bf16[8,64,984]{2,1,0:T(8,128)(2,1)} %get-tuple-element.38), channel_id=1, source_target_pairs={{0,16},{16,0},{1,17},{17,1},{2,18},{18,2},{3,19},{19,3},{4,20},{20... | collective-permute-start | bytes 3022856 | tf_op jit(solution)/shard_map/ppermute | solution.py:539
  360.6 27.4 %collective-permute-start.8 = (bf16[64,1024]{1,0:T(8,128)(2,1)S(1)}, bf16[64,1024]{1,0:T(8,128)(2,1)S(1)}, u32[]{:S(2)}, u32[]{:S(2)}) collective-permute-start(bf16[64,1024]{1,0:T(8,128)(2,1)S(1)} %fusion.35), channel_id=1, source_target_pairs={{0,16},{16,0},{1,17},{17,1},{2,18},{18,2},{3,19},{19,3},{4,20},{20... | collective-permute-start | bytes 393224 | tf_op jit(solution)/shard_map/ppermute | solution.py:539
  379.0 9.7 %collective-permute-start.10 = (f32[128]{0:T(128)S(1)}, f32[128]{0:T(128)S(1)}, u32[]{:S(2)}, u32[]{:S(2)}) collective-permute-start(f32[128]{0:T(128)S(1)} %slice_reduce_fusion.2), channel_id=1, source_target_pairs={{0,16},{16,0},{1,17},{17,1},{2,18},{18,2},{3,19},{19,3},{4,20},{20... | collective-permute-start | bytes 1544 | tf_op jit(solution)/shard_map/ppermute | solution.py:539
  380.6 15.0 %collective-permute-start.6 = (bf16[8,64,384]{2,1,0:T(8,128)(2,1)S(1)}, bf16[8,64,384]{2,1,0:T(8,128)(2,1)S(1)}, u32[]{:S(2)}, u32[]{:S(2)}) collective-permute-start(bf16[8,64,384]{2,1,0:T(8,128)(2,1)S(1)} %get-tuple-element.36), channel_id=1, source_target_pairs={{0,16},{16,0},{1,17},{17,1},{2,18},{18,2},{3,19},{19,3},{4,20},{20... | collective-permute-start | bytes 1179656 | tf_op jit(solution)/shard_map/ppermute | solution.py:539
  402.8 1.7 copy-start.24
Sparse Core Ops, SparseCore 0:
  34.5 75.7 all-gather.1

commit v4 on v3

--- a/solution.py
+++ b/solution.py
@@ -173,21 +173,26 @@
 
 
 def attend_send_kernel(
-    shards, first, w_qkv, w_out, cos, sin, ffn_blocks,
-    attn_sum, ffn_own, q, k, v, att, lse, part, send1, recv1, ybuf, zbuf, send2, recv2,
+    shards, first, w_qkv, w_out, cos, sin, ffn_blocks, top,
+    attn_sum, ffn_own, top_all, q, k, v, att, lse, part, send1, recv1, ybuf, zbuf, send2, recv2,
+    send3, recv3,
 ):
     env = greet(shards, True)
     spread = spread_moves(ffn_blocks, ffn_own, send2, recv2, [], shards, *env)
     scatter = scatter_moves(part, attn_sum, send1, recv1, [ybuf, zbuf], shards, *env)
+    tops = gather_moves(top, top_all, send3, recv3, [], shards, *env)
+    tops[0]()
     spread[0]()
     attend_kernel(
         visits(env[3], scatter[3], shards),
         first, w_qkv, w_out, cos, sin, part, q, k, v, att, lse,
     )
+    tops[1]()
     scatter[1]()
     spread[1]()
     scatter[2]()
     spread[2]()
+    tops[2]()
 
 
 def attend_back_send_kernel(
@@ -485,32 +490,30 @@
     )
     out_own = lax.all_gather(w_out, "core", axis=0, tiled=True)
 
-    def gather(value):
-        return lax.all_gather(value, CHIPS, axis=0, tiled=True)
-
     normed_one, centered_one, inverse_one = layer_norm(x, gains[0])
     first, qkv_own = exchange(
         shards, 1, ("ag", normed_one.astype(bf16)), ("spread", qkv_blocks)
     )
     qkv_own = qkv_own.reshape(features, 3 * WIDE)
-    top_all = gather(grad_top)
     tokens = first.shape[0]
     cos_np, sin_np = rope_tables(tokens)
     cos = take(jnp.asarray(cos_np), 0, core)
     sin = take(jnp.asarray(sin_np), 0, core)
     narrow = ((tokens, WIDE), bf16)
     own_rows = x.shape[0]
-    attn_sum, ffn_own, q, k, v, att, lse = call(
+    attn_sum, ffn_own, top_all, q, k, v, att, lse = call(
         lambda *refs: attend_send_kernel(shards, *refs),
         2,
         [
             ((own_rows, features), f32), ((chips, 2 * rows, 3 * units), bf16),
+            ((tokens, features), bf16),
             narrow, narrow, narrow, narrow, ((tokens, 2), f32),
         ],
         [((tokens, features), bf16)]
         + scatter_scratch(shards, own_rows, features)
-        + sems(2 * chips),
-        first, qkv_own, out_own, cos, sin, ffn_blocks,
+        + sems(2 * chips)
+        + sems(4 * chips + 1),
+        first, qkv_own, out_own, cos, sin, ffn_blocks, grad_top,
     )
     ffn_own = ffn_own.reshape(features, 3 * units)
     in_own, down_own = ffn_own[:, : 2 * units], ffn_own[:, 2 * units :]

time: 420 us -> 418 us (level)
  waiting for transfers between devices: 13.2 us -> 34.6 us
  between operations: 15.4 us -> 1.85 us
  local copies, waits for them, and re-layouts: 34.1 us -> 29.5 us
    ppermute x4, waiting for transfers between devices: 13.1 us -> 34.6 us  [over_replicas(): lax.ppermute(value, 'replica', [(0, 1), (1, 0)]).astype(f32)]
    pallas_call x2, Pallas kernels: 121 us -> 142 us  [call(): pl.pallas_call(kernel, out_shape=[jax.ShapeDtypeStruct(s, d) for s, d in...]
    pallas_call x6, Pallas kernels: 187 us -> 166 us  [exchange(): pl.pallas_call(lambda *refs: comm_kernel(shards, kinds, *refs), out_shape...]
    unnamed x107 -> x83, local copies, waits for them, and re-layouts: 9.15 us -> 6.36 us
  transfers between devices with their start and end apart: 12 -> 11, of which waited for: 2 -> 3; matrix products, arithmetic and copies ran while one was open for 7% -> 5% of each run, Pallas kernels for 58% -> 15%
where the time goes in v4:
time: 418 us; the launch traced here: 412 us
  Pallas kernels  309 us (74%)
  waiting for transfers between devices  34.6 us (8%)
  local copies, waits for them, and re-layouts  29.5 us (7%)
  other arithmetic  15.5 us (4%)
  matrix products  14.2 us (3%)
  starting transfers between devices  6.03 us (1%)
    pallas_call x6, Pallas kernels, exchange(): pl.pallas_call(lambda *refs: comm_kernel(shards, kinds, *refs), out_shape...  166 us
    pallas_call x2, Pallas kernels, call(): pl.pallas_call(kernel, out_shape=[jax.ShapeDtypeStruct(s, d) for s, d in...  142 us
    ppermute x4, waiting for transfers between devices, over_replicas(): lax.ppermute(value, 'replica', [(0, 1), (1, 0)]).astype(f32)  34.6 us
  transfers between devices with their start and end apart: 11, of which 3 were waited for; matrix products, arithmetic and copies ran while one was open for 5% of the time, Pallas kernels for 15%

profile of v4, /device:TPU:0, one launch (start us, length us, event | category | flops | bytes accessed | tf_op | source)
XLA Modules:
  0.0 412.4 jit_solution(4955754072855041819)
XLA Ops:
  0.7 0.8 pad_maximum_fusion.6
  1.5 0.5 collective-permute-start.1
  1.9 1.0 dynamic-slice_bitcast_fusion.6
  2.9 1.0 dynamic-slice_bitcast_fusion.5
  3.9 0.7 pad_maximum_fusion.3
  4.8 2.1 all_gather.3.refs_2_.refs_3_
  6.9 0.5 reshape.147
  7.5 1.3 reshape.145
  8.8 0.6 copy.58
  9.4 0.6 reshape.146
  10.1 0.3 pad_maximum_fusion.1.refs_5_
  10.4 0.9 copy-done.29
  11.3 0.3 copy-done.30
  11.7 0.9 copy-done.27
  12.9 1.1 reshape.143.refs_1_
  14.0 11.0 %shard_map.161 = bf16[128,128]{1,0:T(8,128)(2,1)S(1)} custom-call(bf16[16,128]{1,0:T(8,128)(2,1)S(1)} %pad.10.refs_0_), custom_call_target="tpu_custom_call" | custom-call | tf_op jit(solution)/shard_map/pallas_call | solution.py:440
  25.3 1.0 slice_bitcast_fusion.3
  27.3 37.1 %shard_map.162 = (bf16[1024,1024]{1,0:T(8,128)(2,1)S(1)}, bf16[8,128,384]{2,1,0:T(8,128)(2,1)S(1)}) custom-call(bf16[128,1024]{1,0:T(8,128)(2,1)S(1)} %fusion.21.refs_0_, bf16[8,64,384]{2,1,0:T(8,128)(2,1)S(1)} %copy-done.4), custom_call_target="tpu_custom_call" | custom-call | tf_op jit(solution)/shard_map/pallas_call | solution.py:440
  64.3 1.3 copy-done
  65.7 71.1 %shard_map.163 = (f32[128,1024]{1,0:T(8,128)S(1)}, bf16[8,128,984]{2,1,0:T(8,128)(2,1)}, bf16[1024,1024]{1,0:T(8,128)(2,1)}, bf16[1024,128]{1,0:T(8,128)(2,1)S(1...) custom-call(bf16[1024,1024]{1,0:T(8,128)(2,1)} %copy-done, ...), custom_call_target="tpu_custom_call" | custom-call | tf_op jit(solution)/shard_map/pallas_call | solution.py:159
  137.2 0.4 copy-done.5
  138.0 36.4 %shard_map.164 = bf16[1024,1024]{1,0:T(8,128)(2,1)S(1)} custom-call(bf16[128,1024]{1,0:T(8,128)(2,1)S(1)} %multiply_convert_fusion.1.refs_0_), custom_call_target="tpu_custom_call" | custom-call | tf_op jit(solution)/shard_map/pallas_call | solution.py:440
  174.5 1.6 fusion.2
  176.1 3.2 multiply_convert_fusion
  179.3 1.7 fusion.29
  181.1 2.6 convolution_convert_fusion.2
  183.7 1.9 convolution_convert_fusion.1.refs_0_
  185.6 1.7 convolution_convert_fusion.3
  187.3 29.2 %shard_map.165 = f32[128,1024]{1,0:T(8,128)S(1)} custom-call(bf16[1024,1024]{1,0:T(8,128)(2,1)S(1)} %convolution_convert_fusion.1.refs_0_), custom_call_target="tpu_custom_call" | custom-call | tf_op jit(solution)/shard_map/pallas_call | solution.py:440
  216.5 0.3 multiply_reduce_fusion
  216.8 3.0 pad_maximum_fusion
  219.9 3.9 copy.42
  223.8 1.3 dynamic-slice_bitcast_fusion
  225.3 1.0 fusion.39
  226.3 34.8 %shard_map.166.refs_0_ = bf16[1024,1024]{1,0:T(8,128)(2,1)S(1)} custom-call(bf16[128,1024]{1,0:T(8,128)(2,1)S(1)} %get-tuple-element.52.refs_0_), custom_call_target="tpu_custom_call" | custom-call | tf_op jit(solution)/shard_map/pallas_call | solution.py:440
  261.2 4.7 %convolution_convert_fusion.refs_11_ = bf16[1024,1024]{1,0:T(8,128)(2,1)} fusion(bf16[1024,328]{0,1:T(8,128)(2,1)S(1)} %copy-done.25, bf16[1024,984]{1,0:T(8,128)(2,1)} %bitcast.112), kind=kOutput, calls=%fused_computation.6 | convolution fusion | flops 688914432 | bytes 3555328 | tf_op jit(solution)/shard_map/dot_general | solution.py:42
  266.0 1.4 fusion.refs_12_
  267.5 71.4 %shard_map.167 = (f32[128,1024]{1,0:T(8,128)S(1)}, f32[128,1024]{1,0:T(8,128)S(1)}, bf16[8,64,984]{2,1,0:T(8,128)(2,1)}, bf16[1024,384]{1,0:T(8,128)(2,1)S(1)}, bf16[128,1024]{1,0:T(8,128)(2,1)S(1)}) custom-call(bf16[1024,1024]{1,0:T(8,128)(2,1)} %copy-done.1, bf16[1024,1024]{1,0:T(8,128)(2,1)} %copy-done, bf16[1024,384]{1,0:T(8,128)(2,1)S(1)} %bitcast.92, ...), custom_call_target="tpu_custom_call" | custom-call | tf_op jit(solution)/shard_map/pallas_call | solution.py:159
  339.0 0.6 copy-done.15
  339.6 0.3 fusion.27
  340.1 0.9 dynamic-slice_bitcast_fusion.4
  341.0 0.6 collective-permute-start.7
  342.0 0.5 collective-permute-start.4
  342.5 1.5 collective-permute-start.9
  344.1 0.6 collective-permute-start.8
  344.8 25.9 %collective-permute-done.8 = bf16[64,1024]{1,0:T(8,128)(2,1)S(1)} collective-permute-done((bf16[64,1024]{1,0:T(8,128)(2,1)S(1)}, bf16[64,1024]{1,0:T(8,128)(2,1)S(1)}, u32[]{:S(2)}, u32[]{:S(2)}) %collective-permute-start.8) | collective-permute-done | bytes 131104 | tf_op jit(solution)/shard_map/ppermute | solution.py:542
  370.7 0.7 convert_add_fusion.6
  371.6 17.6 %shard_map.168 = (bf16[8,64,384]{2,1,0:T(8,128)(2,1)S(1)}, f32[8,8,128]{2,1,0:T(8,128)S(1)}) custom-call(bf16[8,64,384]{2,1,0:T(8,128)(2,1)S(1)} %fusion.11.refs_0_, f32[8,8,128]{2,1,0:T(8,128)S(1)} %broadcast_in_dim.5.refs_1_), custom_call_target="tpu_custom_call" | custom-call | tf_op jit(solution)/shard_map/pallas_call | solution.py:440
  389.2 1.6 collective-permute-start.10
  390.8 0.5 collective-permute-start.6
  391.3 0.8 slice_bitcast_fusion.1
  392.1 0.7 collective-permute-done.10
  392.8 0.6 fusion.41
  393.4 8.0 %collective-permute-done.6 = bf16[8,64,384]{2,1,0:T(8,128)(2,1)S(1)} collective-permute-done((bf16[8,64,384]{2,1,0:T(8,128)(2,1)S(1)}, bf16[8,64,384]{2,1,0:T(8,128)(2,1)S(1)}, u32[]{:S(2)}, u32[]{:S(2)}) %collective-permute-start.6) | collective-permute-done | bytes 393248 | tf_op jit(solution)/shard_map/ppermute | solution.py:542
  401.5 0.3 reshape.151
  401.8 0.5 copy.46
  402.3 1.0 copy.57
  403.3 1.9 convert_add_fusion.1
  405.2 1.2 slice_bitcast_fusion
  406.5 1.2 reshape.154
  407.8 0.9 copy.47
  408.7 1.7 reshape.155
  410.4 0.5 copy.48
  410.8 1.1 reshape.156
  (133 shorter events, 4.1 us)
Async XLA Ops:
  0.6 4.1 copy-start.38
  0.6 4.1 copy-start.39
  0.7 4.1 %copy-start.31 = (bf16[64,1024]{1,0:T(8,128)(2,1)S(1)}, bf16[64,1024]{1,0:T(8,128)(2,1)}, u32[]{:S(2)}) copy-start(bf16[64,1024]{1,0:T(8,128)(2,1)} %param.13) | copy-start | bytes 393220
  0.7 6.2 %copy-start.28 = (bf16[2624,64]{0,1:T(8,128)(2,1)S(1)}, bf16[2624,64]{0,1:T(8,128)(2,1)}, u32[]{:S(2)}) copy-start(bf16[2624,64]{0,1:T(8,128)(2,1)} %param.15) | copy-start | bytes 1007620
  1.5 12.5 %collective-permute-start.1 = (bf16[128]{0:T(256)(128)(2,1)S(1)}, bf16[128]{0:T(256)(128)(2,1)S(1)}, u32[]{:S(2)}, u32[]{:S(2)}) collective-permute-start(bf16[128]{0:T(256)(128)(2,1)S(1)} %pad_maximum_fusion.6), channel_id=1, source_target_pairs={{0,1},{1,0},{2,3},{3,2},{4,5},{5,4},{6,7},{7,6},{8,9},{9,8},{10,11... | collective-permute-start | bytes 776 | tf_op jit(solution)/shard_map/ppermute | solution.py:458
  3.9 3.5 copy-start.26
  4.7 20.6 %collective-permute-start = (bf16[2,64,1024]{2,1,0:T(8,128)(2,1)}, bf16[2,64,1024]{2,1,0:T(8,128)(2,1)}, u32[]{:S(2)}, u32[]{:S(2)}) collective-permute-start(bf16[2,64,1024]{2,1,0:T(8,128)(2,1)} %pad_maximum_fusion.3), channel_id=1, source_target_pairs={{0,1},{1,0},{2,3},{3,2},{4,5},{5,4},{6,7},{7,6},{8,9},{9,8},{10,11... | collective-permute-start | bytes 786440 | tf_op jit(solution)/shard_map/ppermute | solution.py:458
  6.9 58.8 %copy-start.2 = (bf16[128,1024]{1,0:T(8,128)(2,1)}, bf16[128,1024]{1,0:T(8,128)(2,1)S(1)}, u32[]{:S(2)}) copy-start(bf16[128,1024]{1,0:T(8,128)(2,1)S(1)} %all_gather.3.refs_2_.refs_3_) | copy-start | bytes 786436
  10.1 1.2 copy-start.29
  10.1 1.5 copy-start.30
  11.6 1.0 copy-start.27
  25.3 2.0 copy-start.4
  26.3 0.6 copy-start.22
  26.5 0.5 copy-start.32
  26.7 0.5 copy-start.34
  64.3 1.3 copy-start
  136.7 0.8 copy-start.5
  136.7 0.9 copy-start.7
  136.8 0.9 copy-start.9
  136.8 1.0 copy-start.11
  136.8 1.1 copy-start.13
  136.9 88.3 %copy-start.17 = (f32[128,1024]{1,0:T(8,128)}, f32[128,1024]{1,0:T(8,128)S(1)}, u32[]{:S(2)}) copy-start(f32[128,1024]{1,0:T(8,128)S(1)} %get-tuple-element.55) | copy-start | bytes 1572868
  138.0 36.5 %copy-start.36 = (bf16[8,128,984]{2,1,0:T(8,128)(2,1)S(1)}, bf16[8,128,984]{2,1,0:T(8,128)(2,1)}, u32[]{:S(2)}) copy-start(bf16[8,128,984]{2,1,0:T(8,128)(2,1)} %get-tuple-element.28) | copy-start | bytes 6045700
  176.1 3.2 copy-start.37
  179.3 6.2 %copy-start.24 = (bf16[1024,328]{0,1:T(8,128)(2,1)}, bf16[1024,328]{0,1:T(8,128)(2,1)S(1)}, u32[]{:S(2)}) copy-start(bf16[1024,328]{0,1:T(8,128)(2,1)S(1)} %get-tuple-element.50) | copy-start | bytes 2015236
  223.8 1.4 copy-start.23
  225.2 40.8 %collective-permute-start.2 = (bf16[8,64,984]{2,1,0:T(8,128)(2,1)S(1)}, bf16[8,64,984]{2,1,0:T(8,128)(2,1)S(1)}, u32[]{:S(2)}, u32[]{:S(2)}) collective-permute-start(bf16[8,64,984]{2,1,0:T(8,128)(2,1)S(1)} %dynamic-slice_bitcast_fusion), channel_id=1, source_target_pairs={{0,1},{1,0},{2,3},{3,2},{4,5},{5,4},{6,7},{7,6},{8,9},{9,8},{10,11... | collective-permute-start | bytes 3022856 | tf_op jit(solution)/shard_map/ppermute | solution.py:458
  226.3 34.8 %copy-start.25 = (bf16[1024,328]{0,1:T(8,128)(2,1)S(1)}, bf16[1024,328]{0,1:T(8,128)(2,1)}, u32[]{:S(2)}) copy-start(bf16[1024,328]{0,1:T(8,128)(2,1)} %copy-done.24) | copy-start | bytes 2015236
  261.2 4.8 %copy-start.1 = (bf16[1024,1024]{1,0:T(8,128)(2,1)}, bf16[1024,1024]{1,0:T(8,128)(2,1)S(1)}, u32[]{:S(2)}) copy-start(bf16[1024,1024]{1,0:T(8,128)(2,1)S(1)} %shard_map.166.refs_0_) | copy-start | bytes 6291460
  261.2 4.8 %copy-start.19 = (bf16[1024,984]{1,0:T(8,128)(2,1)S(1)}, bf16[1024,984]{1,0:T(8,128)(2,1)}, u32[]{:S(2)}) copy-start(bf16[1024,984]{1,0:T(8,128)(2,1)} %copy.42) | copy-start | bytes 6045700
  265.9 1.5 copy-start.3
  265.9 1.5 copy-start.6
  265.9 1.5 copy-start.8
  265.9 1.5 copy-start.10
  266.0 1.5 copy-start.12
  266.0 1.5 copy-start.14
  267.4 71.5 %copy-start.18 = (f32[128,1024]{1,0:T(8,128)S(1)}, f32[128,1024]{1,0:T(8,128)}, u32[]{:S(2)}) copy-start(f32[128,1024]{1,0:T(8,128)} %copy-done.17) | copy-start | bytes 1572868
  267.5 72.1 %copy-start.33 = (f32[128]{0:T(128)S(1)}, f32[128]{0:T(128)}, u32[]{:S(2)}) copy-start(f32[128]{0:T(128)} %copy-done.32) | copy-start | bytes 1540
  267.5 72.1 %copy-start.35 = (f32[128]{0:T(128)S(1)}, f32[128]{0:T(128)}, u32[]{:S(2)}) copy-start(f32[128]{0:T(128)} %copy-done.34) | copy-start | bytes 1540
  338.9 0.7 copy-start.15
  338.9 2.7 copy-start.21
  340.0 4.7 %collective-permute-start.5 = (f32[2,8,64]{2,1,0:T(8,128)S(1)}, f32[2,8,64]{2,1,0:T(8,128)S(1)}, u32[]{:S(2)}, u32[]{:S(2)}) collective-permute-start(f32[2,8,64]{2,1,0:T(8,128)S(1)} %bitcast.110), channel_id=1, source_target_pairs={{0,1},{1,0},{2,3},{3,2},{4,5},{5,4},{6,7},{7,6},{8,9},{9,8},{10,11... | collective-permute-start | bytes 12296 | tf_op jit(solution)/shard_map/ppermute | solution.py:458
  341.0 3.1 collective-permute-start.7
  341.5 2.5 copy-start.16
  341.8 29.6 %collective-permute-start.3 = (bf16[2,64,1024]{2,1,0:T(8,128)(2,1)S(1)}, bf16[2,64,1024]{2,1,0:T(8,128)(2,1)S(1)}, u32[]{:S(2)}, u32[]{:S(2)}) collective-permute-start(bf16[2,64,1024]{2,1,0:T(8,128)(2,1)S(1)} %get-tuple-element.61), channel_id=1, source_target_pairs={{0,1},{1,0},{2,3},{3,2},{4,5},{5,4},{6,7},{7,6},{8,9},{9,8},{10,11... | collective-permute-start | bytes 786440 | tf_op jit(solution)/shard_map/ppermute | solution.py:458
  342.0 29.5 %collective-permute-start.4 = (bf16[8,64,384]{2,1,0:T(8,128)(2,1)S(1)}, bf16[8,64,384]{2,1,0:T(8,128)(2,1)S(1)}, u32[]{:S(2)}, u32[]{:S(2)}) collective-permute-start(bf16[8,64,384]{2,1,0:T(8,128)(2,1)S(1)} %dynamic-slice_bitcast_fusion.3), channel_id=1, source_target_pairs={{0,1},{1,0},{2,3},{3,2},{4,5},{5,4},{6,7},{7,6},{8,9},{9,8},{10,11... | collective-permute-start | bytes 1179656 | tf_op jit(solution)/shard_map/ppermute | solution.py:458
  342.5 60.8 %collective-permute-start.9 = (bf16[8,64,984]{2,1,0:T(8,128)(2,1)}, bf16[8,64,984]{2,1,0:T(8,128)(2,1)}, u32[]{:S(2)}, u32[]{:S(2)}) collective-permute-start(bf16[8,64,984]{2,1,0:T(8,128)(2,1)} %get-tuple-element.40), channel_id=1, source_target_pairs={{0,16},{16,0},{1,17},{17,1},{2,18},{18,2},{3,19},{19,3},{4,20},{20... | collective-permute-start | bytes 3022856 | tf_op jit(solution)/shard_map/ppermute | solution.py:542
  344.1 26.6 %collective-permute-start.8 = (bf16[64,1024]{1,0:T(8,128)(2,1)S(1)}, bf16[64,1024]{1,0:T(8,128)(2,1)S(1)}, u32[]{:S(2)}, u32[]{:S(2)}) collective-permute-start(bf16[64,1024]{1,0:T(8,128)(2,1)S(1)} %fusion.35), channel_id=1, source_target_pairs={{0,16},{16,0},{1,17},{17,1},{2,18},{18,2},{3,19},{19,3},{4,20},{20... | collective-permute-start | bytes 393224 | tf_op jit(solution)/shard_map/ppermute | solution.py:542
  389.2 3.6 collective-permute-start.10
  390.8 10.6 %collective-permute-start.6 = (bf16[8,64,384]{2,1,0:T(8,128)(2,1)S(1)}, bf16[8,64,384]{2,1,0:T(8,128)(2,1)S(1)}, u32[]{:S(2)}, u32[]{:S(2)}) collective-permute-start(bf16[8,64,384]{2,1,0:T(8,128)(2,1)S(1)} %get-tuple-element.38), channel_id=1, source_target_pairs={{0,16},{16,0},{1,17},{17,1},{2,18},{18,2},{3,19},{19,3},{4,20},{20... | collective-permute-start | bytes 1179656 | tf_op jit(solution)/shard_map/ppermute | solution.py:542
  408.7 1.7 copy-start.20
